TPU v7x, 32 devices: a whole 2x2x4 slice. The times are simulated.
32 devices in a mesh: fsdp: 16 (over z, x, core), tp: 2 (over y).
Axes of the slice: x: 2, y: 2, z: 4, core: 2. Of those that a mesh axis runs over, the one named last changes fastest.
Arguments:
- inputs: bfloat16 [16384, 1152], P(('fsdp', 'tp')), may hold values from -6 to 6
- conditions: bfloat16 [16, 1152], P('fsdp'), may hold values from -6 to 6
- modulation_weight: bfloat16 [1152, 6, 1152], P('fsdp', None, 'tp'), may hold values from -0.1875 to 0.1875
- modulation_bias: bfloat16 [6, 1152], P(None, 'tp'), may hold values from -3 to 3
- attention_weight: bfloat16 [1152, 3, 1152], P('fsdp', None, 'tp'), may hold values from -0.1875 to 0.1875
- attention_bias: bfloat16 [2, 1152], P(None, 'tp'), may hold values from -3 to 3
- output_weight: bfloat16 [1152, 1152], P('tp', 'fsdp'), may hold values from -1.5 to 1.5
- output_bias: bfloat16 [1152], replicated, may hold values from -1.75 to 1.75
- up_weight: bfloat16 [1152, 4608], P('fsdp', 'tp'), may hold values from -0.1875 to 0.1875
- up_bias: bfloat16 [4608], P('tp'), may hold values from -3 to 3
- down_weight: bfloat16 [4608, 1152], P('tp', 'fsdp'), may hold values from -0.09375 to 0.09375
- down_bias: bfloat16 [1152], replicated, may hold values from -1.75 to 1.75
- cotangent: bfloat16 [16384, 1152], P(('fsdp', 'tp')), may hold values from -6 to 6
Outputs:
- outputs: bfloat16 [16384, 1152], P(('fsdp', 'tp'))
- grad_inputs: float32 [16384, 1152], P(('fsdp', 'tp'))
- grad_conditions: float32 [16, 1152], P('fsdp')
- grad_modulation_weight: float32 [1152, 6, 1152], P('fsdp', None, 'tp')
- grad_modulation_bias: float32 [6, 1152], P(None, 'tp')
- grad_attention_weight: float32 [1152, 3, 1152], P('fsdp', None, 'tp')
- grad_attention_bias: float32 [2, 1152], P(None, 'tp')
- grad_output_weight: float32 [1152, 1152], P('tp', 'fsdp')
- grad_output_bias: float32 [1152], replicated
- grad_up_weight: float32 [1152, 4608], P('fsdp', 'tp')
- grad_up_bias: float32 [4608], P('tp')
- grad_down_weight: float32 [4608, 1152], P('tp', 'fsdp')
- grad_down_bias: float32 [1152], replicated
All inputs are finite; a program needn't handle non-finite values.
Results may differ from a plain program's by a relative error of at most 0.02.
The roundings to bfloat16 on the way count: a program that leaves them out, or rounds other values in their place, can miss the bound.
Values may be sent and summed in bfloat16 or wider, within the bound.
No kernel may reach another device: no remote copies, remote signals or barrier semaphores. Data moves between devices by JAX's collectives and lax.ppermute only.
A program may use at most 192 MiB of HBM per device.

v0:
```python
import math

import jax
import jax.numpy as jnp
from jax import lax
from jax.sharding import PartitionSpec as P

HD = 72


EPS = 1e-06
HIGH = lax.Precision.HIGHEST


def normalize(values):
    centred = values - jnp.mean(values, axis=-1, keepdims=True)
    inverse = lax.rsqrt(jnp.mean(centred * centred, axis=-1, keepdims=True) + EPS)
    return (centred * inverse, inverse)


def normalize_back(incoming, normed, inverse):
    first_mean = jnp.mean(incoming, axis=-1, keepdims=True)
    second_mean = jnp.mean(incoming * normed, axis=-1, keepdims=True)
    return inverse * (incoming - first_mean - normed * second_mean)


def modulate(normed, shift, scale):
    return (normed * (1.0 + scale) + shift).astype(jnp.bfloat16)


def silu_slope(values):
    sigmoid = jax.nn.sigmoid(values)
    return sigmoid * (1.0 + values * (1.0 - sigmoid))


def spread_rows(selector, table):
    return jnp.dot(selector, table, precision=HIGH)


def collect_rows(selector, values):
    return jnp.dot(selector.T, values, precision=HIGH)


def place_columns(piece, rank, count):
    width = piece.shape[-1]
    whole = jnp.zeros(piece.shape[:-1] + (width * count,), jnp.float32)
    return lax.dynamic_update_slice_in_dim(whole, piece, rank * width, piece.ndim - 1)


def take_columns(whole, rank, count):
    width = whole.shape[-1] // count
    return lax.dynamic_slice_in_dim(whole, rank * width, width, whole.ndim - 1)


def place_rows(piece, rank, count):
    height = piece.shape[0]
    whole = jnp.zeros((height * count,) + piece.shape[1:], jnp.float32)
    return lax.dynamic_update_slice_in_dim(whole, piece, rank * height, 0)


def take_rows(whole, rank, count):
    height = whole.shape[0] // count
    return lax.dynamic_slice_in_dim(whole, rank * height, height, 0)


def fetch_weights(shards):
    return (
        lax.all_gather(shards[0], "fsdp", axis=0, tiled=True),
        lax.all_gather(shards[1], "fsdp", axis=0, tiled=True),
        lax.all_gather(shards[2], "fsdp", axis=0, tiled=True),
        lax.all_gather(shards[3], "fsdp", axis=1, tiled=True),
        lax.all_gather(shards[4], "fsdp", axis=1, tiled=True),
    )


def attention_gather(normed_low):
    return lax.all_gather(normed_low, "tp", axis=0, tiled=True)


def feed_gather(normed_low):
    return lax.all_gather(normed_low, "tp", axis=0, tiled=True)


def attend_latent(packed):
    length = packed.shape[0]
    block = min(512, length)
    scale = 1.0 / math.sqrt(packed.shape[3])
    key_rows = packed[:, 1]
    value_rows = packed[:, 2]
    results = []
    log_totals = []
    for offset in range(0, length, block):
        queries = packed[offset : offset + block, 0]
        scores = (
            jnp.einsum("qhe,khe->hqk", queries, key_rows, preferred_element_type=jnp.float32)
            * scale
        )
        row_max = jnp.max(scores, axis=-1, keepdims=True)
        shares = jnp.exp(scores - row_max)
        totals = jnp.sum(shares, axis=-1, keepdims=True)
        shares_low = (shares / totals).astype(jnp.bfloat16)
        results.append(
            jnp.einsum("hqk,khe->qhe", shares_low, value_rows, preferred_element_type=jnp.float32)
        )
        log_totals.append((row_max + jnp.log(totals))[:, :, 0])
    return (jnp.concatenate(results, axis=0), jnp.concatenate(log_totals, axis=1))


def attend_back(items):
    packed, upstream, log_totals = items
    length = packed.shape[0]
    block = min(512, length)
    scale = 1.0 / math.sqrt(packed.shape[3])
    all_queries = packed[:, 0]
    key_rows = packed[:, 1]
    value_rows = packed[:, 2]
    key_grads = jnp.zeros(key_rows.shape, jnp.float32)
    value_grads = jnp.zeros(value_rows.shape, jnp.float32)
    query_grads = []
    for offset in range(0, length, block):
        queries = all_queries[offset : offset + block]
        incoming = upstream[offset : offset + block]
        scores = (
            jnp.einsum("qhe,khe->hqk", queries, key_rows, preferred_element_type=jnp.float32)
            * scale
        )
        shares = jnp.exp(scores - log_totals[:, offset : offset + block, None])
        share_grads = jnp.einsum(
            "qhe,khe->hqk", incoming, value_rows, preferred_element_type=jnp.float32
        )
        inner = jnp.sum(share_grads * shares, axis=-1, keepdims=True)
        score_grads = (shares * (share_grads - inner)).astype(jnp.bfloat16)
        query_grads.append(
            jnp.einsum("hqk,khe->qhe", score_grads, key_rows, preferred_element_type=jnp.float32)
            * scale
        )
        key_grads = (
            key_grads
            + jnp.einsum("hqk,qhe->khe", score_grads, queries, preferred_element_type=jnp.float32)
            * scale
        )
        value_grads = value_grads + jnp.einsum(
            "hqk,qhe->khe",
            shares.astype(jnp.bfloat16),
            incoming,
            preferred_element_type=jnp.float32,
        )
    return jnp.stack([jnp.concatenate(query_grads, axis=0), key_grads, value_grads], axis=1)


def per_device(
    inputs,
    conditions,
    modulation_weight,
    modulation_bias,
    attention_weight,
    attention_bias,
    output_weight,
    output_bias,
    up_weight,
    up_bias,
    down_weight,
    down_bias,
    cotangent,
):
    tensor_size = lax.axis_size("tp")
    tensor_rank = lax.axis_index("tp")
    fsdp_size = lax.axis_size("fsdp")
    fsdp_rank = lax.axis_index("fsdp")
    local_rows = inputs.shape[0]
    latents = conditions.shape[0]
    group_rows = local_rows * tensor_size
    length = group_rows // latents
    head_cols = attention_weight.shape[2]
    heads = head_cols // HD
    positions = tensor_rank * local_rows + jnp.arange(local_rows, dtype=jnp.int32)
    selector = (
        positions[:, None] // length == jnp.arange(latents, dtype=jnp.int32)[None, :]
    ).astype(jnp.float32)
    shards = (modulation_weight, attention_weight, up_weight, output_weight, down_weight)
    modulation_all, attention_all, up_all, output_all, down_all = fetch_weights(shards)
    condition_values = conditions.astype(jnp.float32)
    silu_low = jax.nn.silu(condition_values).astype(jnp.bfloat16)
    own_columns = jnp.einsum(
        "ld,dkc->lkc", silu_low, modulation_all, preferred_element_type=jnp.float32
    ) + modulation_bias.astype(jnp.float32)
    modulation = lax.all_gather(own_columns, "tp", axis=2, tiled=True)
    shift_one = spread_rows(selector, modulation[:, 0])
    scale_one = spread_rows(selector, modulation[:, 1])
    gate_one = spread_rows(selector, modulation[:, 2])
    shift_two = spread_rows(selector, modulation[:, 3])
    scale_two = spread_rows(selector, modulation[:, 4])
    gate_two = spread_rows(selector, modulation[:, 5])
    input_values = inputs.astype(jnp.float32)
    first_normed, first_inverse = normalize(input_values)
    first_all = attention_gather(modulate(first_normed, shift_one, scale_one))
    bias_rows = attention_bias.astype(jnp.float32)
    packed_bias = jnp.stack([bias_rows[0], jnp.zeros_like(bias_rows[0]), bias_rows[1]])
    projected = (
        jnp.einsum("rd,dkc->rkc", first_all, attention_all, preferred_element_type=jnp.float32)
        + packed_bias
    )
    packed = projected.astype(jnp.bfloat16).reshape(latents, length, 3, heads, HD)
    heads_out, log_totals = lax.map(attend_latent, packed)
    heads_low = heads_out.reshape(group_rows, head_cols).astype(jnp.bfloat16)
    attention = lax.psum_scatter(
        jnp.dot(
            lax.slice_in_dim(heads_low, 0, local_rows * lax.axis_size("tp"), axis=0),
            output_all,
            preferred_element_type=jnp.float32,
        ),
        "tp",
        scatter_dimension=0,
        tiled=True,
    ) + output_bias.astype(jnp.float32)
    mid = input_values + gate_one * attention
    second_normed, second_inverse = normalize(mid)
    second_all = feed_gather(modulate(second_normed, shift_two, scale_two))
    pre = jnp.dot(second_all, up_all, preferred_element_type=jnp.float32) + up_bias.astype(
        jnp.float32
    )
    act_low = jax.nn.gelu(pre, approximate=True).astype(jnp.bfloat16)
    feed = lax.psum_scatter(
        jnp.dot(
            lax.slice_in_dim(act_low, 0, local_rows * lax.axis_size("tp"), axis=0),
            down_all,
            preferred_element_type=jnp.float32,
        ).astype(jnp.bfloat16),
        "tp",
        scatter_dimension=0,
        tiled=True,
    ).astype(jnp.float32) + down_bias.astype(jnp.float32)
    outputs = (mid + gate_two * feed).astype(jnp.bfloat16)
    upstream = cotangent.astype(jnp.float32)
    feed_low = (gate_two * upstream).astype(jnp.bfloat16)
    feed_grad_all = lax.all_gather(feed_low, "tp", axis=0, tiled=True)
    refreshed, held_inputs, held_mid, anchor = lax.optimization_barrier(
        (shards, input_values, mid, feed_grad_all)
    )
    modulation_all, attention_all, up_all, output_all, down_all = fetch_weights(refreshed)
    first_normed, first_inverse = normalize(held_inputs)
    first_all = attention_gather(modulate(first_normed, shift_one, scale_one))
    second_normed, second_inverse = normalize(held_mid)
    second_all = feed_gather(modulate(second_normed, shift_two, scale_two))
    feed_grad_all = anchor
    down_grad = jnp.einsum("rh,rd->hd", act_low, feed_grad_all, preferred_element_type=jnp.float32)
    act_grad = jnp.einsum("rd,hd->rh", feed_grad_all, down_all, preferred_element_type=jnp.float32)
    gelu_out, gelu_back = jax.vjp(lambda inner: jax.nn.gelu(inner, approximate=True), pre)
    pre_low = gelu_back(act_grad)[0].astype(jnp.bfloat16)
    up_grad = jnp.einsum("rd,rh->dh", second_all, pre_low, preferred_element_type=jnp.float32)
    second_grad = lax.psum_scatter(
        jnp.einsum(
            "rh,dh->rd",
            lax.slice_in_dim(pre_low, 0, local_rows * lax.axis_size("tp"), axis=0),
            up_all,
            preferred_element_type=jnp.float32,
        ).astype(jnp.bfloat16),
        "tp",
        scatter_dimension=0,
        tiled=True,
    ).astype(jnp.float32)
    shift_two_grad = collect_rows(selector, second_grad)
    scale_two_grad = collect_rows(selector, second_grad * second_normed)
    gate_two_grad = collect_rows(selector, upstream * feed)
    mid_grad = upstream + normalize_back(
        second_grad * (1.0 + scale_two), second_normed, second_inverse
    )
    gate_one_grad = collect_rows(selector, mid_grad * attention)
    attention_low = (gate_one * mid_grad).astype(jnp.bfloat16)
    attention_grad_all = lax.all_gather(attention_low, "tp", axis=0, tiled=True)
    output_grad = jnp.einsum(
        "rc,rd->cd", heads_low, attention_grad_all, preferred_element_type=jnp.float32
    )
    heads_grad = jnp.einsum(
        "rd,cd->rc", attention_grad_all, output_all, preferred_element_type=jnp.float32
    ).astype(jnp.bfloat16)
    packed_grad = lax.map(
        attend_back, (packed, heads_grad.reshape(latents, length, heads, HD), log_totals)
    )
    packed_low = packed_grad.reshape(group_rows, 3, head_cols).astype(jnp.bfloat16)
    attention_grad = jnp.einsum(
        "rd,rkc->dkc", first_all, packed_low, preferred_element_type=jnp.float32
    )
    first_grad = lax.psum_scatter(
        jnp.einsum(
            "rkc,dkc->rd",
            lax.slice_in_dim(packed_low, 0, local_rows * lax.axis_size("tp"), axis=0),
            attention_all,
            preferred_element_type=jnp.float32,
        ).astype(jnp.bfloat16),
        "tp",
        scatter_dimension=0,
        tiled=True,
    ).astype(jnp.float32)
    shift_one_grad = collect_rows(selector, first_grad)
    scale_one_grad = collect_rows(selector, first_grad * first_normed)
    grad_inputs = mid_grad + normalize_back(
        first_grad * (1.0 + scale_one), first_normed, first_inverse
    )
    modulation_parts = jnp.stack(
        [
            shift_one_grad,
            scale_one_grad,
            gate_one_grad,
            shift_two_grad,
            scale_two_grad,
            gate_two_grad,
        ],
        axis=1,
    )
    modulation_summed = lax.psum_scatter(modulation_parts, "tp", scatter_dimension=2, tiled=True)
    modulation_low = modulation_summed.astype(jnp.bfloat16)
    modulation_grad = jnp.einsum(
        "ld,lkc->dkc", silu_low, modulation_low, preferred_element_type=jnp.float32
    )
    silu_part = jnp.einsum(
        "lkc,dkc->ld", modulation_low, modulation_all, preferred_element_type=jnp.float32
    )
    (
        grad_modulation_weight,
        grad_attention_weight,
        grad_up_weight,
        grad_output_weight,
        grad_down_weight,
    ) = (
        lax.psum_scatter(
            modulation_grad.astype(jnp.bfloat16), "fsdp", scatter_dimension=0, tiled=True
        ).astype(jnp.float32),
        lax.psum_scatter(
            attention_grad.astype(jnp.bfloat16), "fsdp", scatter_dimension=0, tiled=True
        ).astype(jnp.float32),
        lax.psum_scatter(
            up_grad.astype(jnp.bfloat16), "fsdp", scatter_dimension=0, tiled=True
        ).astype(jnp.float32),
        lax.psum_scatter(
            output_grad.astype(jnp.bfloat16), "fsdp", scatter_dimension=1, tiled=True
        ).astype(jnp.float32),
        lax.psum_scatter(
            down_grad.astype(jnp.bfloat16), "fsdp", scatter_dimension=1, tiled=True
        ).astype(jnp.float32),
    )
    qv_part = jnp.stack(
        [
            jnp.sum(packed_low[:, 0], axis=0, dtype=jnp.float32),
            jnp.sum(packed_low[:, 2], axis=0, dtype=jnp.float32),
        ]
    )
    up_part = jnp.sum(pre_low, axis=0, dtype=jnp.float32)
    modulation_part = jnp.sum(modulation_low, axis=0, dtype=jnp.float32)
    output_part = jnp.sum(attention_low, axis=0, dtype=jnp.float32)
    down_part = jnp.sum(feed_low, axis=0, dtype=jnp.float32)
    qv_total, up_total, modulation_total, grad_output_bias, grad_down_bias, silu_total = lax.psum(
        (
            place_columns(qv_part, tensor_rank, tensor_size),
            place_columns(up_part, tensor_rank, tensor_size),
            place_columns(modulation_part, tensor_rank, tensor_size),
            output_part,
            down_part,
            place_rows(silu_part, fsdp_rank, fsdp_size),
        ),
        ("fsdp", "tp"),
    )
    grad_attention_bias = take_columns(qv_total, tensor_rank, tensor_size)
    grad_up_bias = take_columns(up_total, tensor_rank, tensor_size)
    grad_modulation_bias = take_columns(modulation_total, tensor_rank, tensor_size)
    grad_conditions = take_rows(silu_total, fsdp_rank, fsdp_size) * silu_slope(condition_values)
    return (
        outputs,
        grad_inputs,
        grad_conditions,
        grad_modulation_weight,
        grad_modulation_bias,
        grad_attention_weight,
        grad_attention_bias,
        grad_output_weight,
        grad_output_bias,
        grad_up_weight,
        grad_up_bias,
        grad_down_weight,
        grad_down_bias,
    )


def solution(mesh):
    placed = (
        P(("fsdp", "tp"), None),
        P("fsdp", None),
        P("fsdp", None, "tp"),
        P(None, "tp"),
        P("fsdp", None, "tp"),
        P(None, "tp"),
        P("tp", "fsdp"),
        P(),
        P("fsdp", "tp"),
        P("tp"),
        P("tp", "fsdp"),
        P(),
        P(("fsdp", "tp"), None),
    )
    return jax.shard_map(
        per_device,
        mesh=mesh,
        in_specs=placed,
        out_specs=(
            P(("fsdp", "tp"), None),
            P(("fsdp", "tp"), None),
            P("fsdp", None),
            P("fsdp", None, "tp"),
            P(None, "tp"),
            P("fsdp", None, "tp"),
            P(None, "tp"),
            P("tp", "fsdp"),
            P(),
            P("fsdp", "tp"),
            P("tp"),
            P("tp", "fsdp"),
            P(),
        ),
        check_vma=False,
    )
```

profile of v0, /device:TPU:0, one launch (start us, length us, event | category | flops | bytes accessed | tf_op | source)
XLA Modules:
  0.0 1712.9 jit_solution(1686140433479574405)
XLA Ops:
  11.4 79.4 %all-gather.19.cloned.1.call-done = bf16[1152,6,576]{2,0,1:T(8,128)(2,1)} async-done(((bf16[72,6,576]{2,0,1:T(8,128)(2,1)}), bf16[1152,6,576]{2,0,1:T(8,128)(2,1)}) %all-gather.19.cloned.1.call-update) | async-done | bytes 7962640 | tf_op jit(solution)/shard_map/all_gather | solution.py:68
  104.1 38.8 %all-gather.23.cloned.1.call-done = bf16[1152,3,576]{2,0,1:T(8,128)(2,1)} async-done(((bf16[72,3,576]{2,0,1:T(8,128)(2,1)}), bf16[1152,3,576]{2,0,1:T(8,128)(2,1)}) %all-gather.23.cloned.1.call-update) | async-done | bytes 3981328 | tf_op jit(solution)/shard_map/all_gather | solution.py:69
  142.9 36.7 %all-gather.21.cloned.1.call-done = bf16[1024,1152]{1,0:T(8,128)(2,1)} async-done(((bf16[512,1152]{1,0:T(8,128)(2,1)}), bf16[1024,1152]{1,0:T(8,128)(2,1)}) %all-gather.21.cloned.1.call-update) | async-done | bytes 2359312 | tf_op jit(solution)/shard_map/all_gather | solution.py:77
  198.2 13.5 fusion.1
  235.8 59.0 %reduce-scatter.17.cloned.1.call-done = f32[512,1152]{1,0:T(8,128)} async-done(((f32[1024,1152]{1,0:T(8,128)}), f32[512,1152]{1,0:T(8,128)}) %reduce-scatter.17.cloned.1.call-update) | async-done | bytes 2359312 | tf_op jit(solution)/shard_map/reduce_scatter | solution.py:206
  301.5 51.9 %all-gather.29.cloned.1.call-done = bf16[1152,2304]{1,0:T(8,128)(2,1)} async-done(((bf16[72,2304]{1,0:T(8,128)(2,1)}), bf16[1152,2304]{1,0:T(8,128)(2,1)}) %all-gather.29.cloned.1.call-update) | async-done | bytes 5308432 | tf_op jit(solution)/shard_map/all_gather | solution.py:70
  353.4 36.9 %all-gather.27.cloned.1.call-done = bf16[1024,1152]{1,0:T(8,128)(2,1)} async-done(((bf16[512,1152]{1,0:T(8,128)(2,1)}), bf16[1024,1152]{1,0:T(8,128)(2,1)}) %all-gather.27.cloned.1.call-update) | async-done | bytes 2359312 | tf_op jit(solution)/shard_map/all_gather | solution.py:81
  402.2 46.8 %all-gather.31.cloned.1.call-done = bf16[2304,1152]{0,1:T(8,128)(2,1)} async-done(((bf16[2304,72]{0,1:T(8,128)(2,1)}), bf16[2304,1152]{0,1:T(8,128)(2,1)}) %all-gather.31.cloned.1.call-update) | async-done | bytes 5308432 | tf_op jit(solution)/shard_map/all_gather | solution.py:72
  449.1 13.4 convolution_convert_fusion.4
  463.8 32.2 %reduce-scatter.19.cloned.1.call-done = bf16[512,1152]{1,0:T(8,128)(2,1)} async-done(((bf16[1024,1152]{1,0:T(8,128)(2,1)}), bf16[512,1152]{1,0:T(8,128)(2,1)}) %reduce-scatter.19.cloned.1.call-update) | async-done | bytes 1179664 | tf_op jit(solution)/shard_map/reduce_scatter | solution.py:223
  502.0 34.6 %all-gather.33.cloned.1.call-done = bf16[1024,1152]{1,0:T(8,128)(2,1)} async-done(((bf16[512,1152]{1,0:T(8,128)(2,1)}), bf16[1024,1152]{1,0:T(8,128)(2,1)}) %all-gather.33.cloned.1.call-update) | async-done | bytes 2359312 | tf_op jit(solution)/shard_map/all_gather | solution.py:236
  537.3 57.9 %all-gather.35.cloned.1.call-done = bf16[2304,1152]{0,1:T(8,128)(2,1)} async-done(((bf16[2304,72]{0,1:T(8,128)(2,1)}), bf16[2304,1152]{0,1:T(8,128)(2,1)}) %all-gather.35.cloned.1.call-update) | async-done | bytes 5308432 | tf_op jit(solution)/shard_map/all_gather | solution.py:72
  595.2 17.1 convert_reduce_fusion
  612.3 39.9 %all-gather.37.cloned.1.call-done = bf16[1152,2304]{1,0:T(8,128)(2,1)} async-done(((bf16[72,2304]{1,0:T(8,128)(2,1)}), bf16[1152,2304]{1,0:T(8,128)(2,1)}) %all-gather.37.cloned.1.call-update) | async-done | bytes 5308432 | tf_op jit(solution)/shard_map/all_gather | solution.py:70
  664.8 31.6 %reduce-scatter.21.cloned.1.call-done = bf16[512,1152]{1,0:T(8,128)(2,1)} async-done(((bf16[1024,1152]{1,0:T(8,128)(2,1)}), bf16[512,1152]{1,0:T(8,128)(2,1)}) %reduce-scatter.21.cloned.1.call-update) | async-done | bytes 1179664 | tf_op jit(solution)/shard_map/reduce_scatter | solution.py:251
  704.3 33.7 %all-gather.41.cloned.1.call-done = bf16[576,1152]{0,1:T(8,128)(2,1)} async-done(((bf16[576,72]{0,1:T(8,128)(2,1)}), bf16[576,1152]{0,1:T(8,128)(2,1)}) %all-gather.41.cloned.1.call-update) | async-done | bytes 1327120 | tf_op jit(solution)/shard_map/all_gather | solution.py:71
  738.0 36.4 %all-gather.39.cloned.1.call-done = bf16[1024,1152]{1,0:T(8,128)(2,1)} async-done(((bf16[512,1152]{1,0:T(8,128)(2,1)}), bf16[1024,1152]{1,0:T(8,128)(2,1)}) %all-gather.39.cloned.1.call-update) | async-done | bytes 2359312 | tf_op jit(solution)/shard_map/all_gather | solution.py:270
  779.1 14.7 multiply_reduce_fusion.1
  826.8 15.9 multiply_convert_fusion.1
  891.1 23.3 %reduce-scatter.23.cloned.1.call-done = bf16[512,1152]{1,0:T(8,128)(2,1)} async-done(((bf16[1024,1152]{1,0:T(8,128)(2,1)}), bf16[512,1152]{1,0:T(8,128)(2,1)}) %reduce-scatter.23.cloned.1.call-update) | async-done | bytes 1179664 | tf_op jit(solution)/shard_map/reduce_scatter | solution.py:284
  947.5 71.0 %all-gather.45.cloned.1.call-done = bf16[1152,6,576]{2,0,1:T(8,128)(2,1)} async-done(((bf16[72,6,576]{2,0,1:T(8,128)(2,1)}), bf16[1152,6,576]{2,0,1:T(8,128)(2,1)}) %all-gather.45.cloned.1.call-update) | async-done | bytes 7962640 | tf_op jit(solution)/shard_map/all_gather | solution.py:68
  1025.3 29.0 %all-gather.49.cloned.1.call-done = bf16[1024,1152]{1,0:T(8,128)(2,1)} async-done(((bf16[512,1152]{1,0:T(8,128)(2,1)}), bf16[1024,1152]{1,0:T(8,128)(2,1)}) %all-gather.49.cloned.1.call-update) | async-done | bytes 2359312 | tf_op jit(solution)/shard_map/all_gather | solution.py:81
  1072.6 19.5 %all-gather.47.cloned.1.call-done = bf16[1024,1152]{1,0:T(8,128)(2,1)} async-done(((bf16[512,1152]{1,0:T(8,128)(2,1)}), bf16[1024,1152]{1,0:T(8,128)(2,1)}) %all-gather.47.cloned.1.call-update) | async-done | bytes 2359312 | tf_op jit(solution)/shard_map/all_gather | solution.py:77
  1100.2 18.2 %copy.39 = bf16[1152,3,576]{2,1,0:T(4,128)(2,1)} copy(bf16[1152,3,576]{2,0,1:T(8,128)(2,1)S(1)} %convolution_convert_fusion.2) | data formatting | bytes 7962624
  1118.4 12.3 reshape.266
  1132.6 43.9 %reduce-scatter.27.cloned.1.call-done = bf16[2304,72]{0,1:T(8,128)(2,1)} async-done(((bf16[2304,1152]{0,1:T(8,128)(2,1)}), bf16[2304,72]{0,1:T(8,128)(2,1)}) %reduce-scatter.27.cloned.1.call-update) | async-done | bytes 331792 | tf_op jit(solution)/shard_map/reduce_scatter | solution.py:338
  1179.4 58.9 %reduce-scatter.33.cloned.1.call-done = bf16[576,72]{0,1:T(8,128)(2,1)} async-done(((bf16[576,1152]{0,1:T(8,128)(2,1)}), bf16[576,72]{0,1:T(8,128)(2,1)}) %reduce-scatter.33.cloned.1.call-update) | async-done | bytes 82960
  1240.3 41.4 %all-reduce.2 = (f32[6,1152]{1,0:T(8,128)S(1)}, f32[2,1152]{1,0:T(2,128)S(1)}, f32[1152]{0:T(1024)}, f32[4608]{0:T(1024)S(1)}, f32[1152]{0:T(1024)}) all-reduce(f32[6,1152]{1,0:T(8,128)S(1)} %dynamic_update_slice.22, f32[2,1152]{1,0:T(2,128)S(1)} %dynamic_update_slice.23, ...), channel_id=1, replica_groups=mesh['fsdp'=16,'tp'=2] {'fsdp','tp'}, use_global_device_ids=true, to_apply=%region_25.26 | all-reduce | flops 16128 | bytes 129024 | tf_op jit(solution)/shard_map/psum | solution.py:352
  1283.7 78.9 %all-reduce.6.cloned.1.call-done = f32[16,1152]{1,0:T(8,128)} async-done(((f32[16,1152]{1,0:T(8,128)}), f32[16,1152]{1,0:T(8,128)}) %all-reduce.6.cloned.1.call-update) | async-done | bytes 73744 | tf_op jit(solution)/shard_map/psum | solution.py:352
  1364.0 85.0 %reduce-scatter.25.cloned.1.call-done = bf16[72,2304]{1,0:T(8,128)(2,1)} async-done(((bf16[1152,2304]{1,0:T(8,128)(2,1)}), bf16[72,2304]{1,0:T(8,128)(2,1)}) %reduce-scatter.25.cloned.1.call-update) | async-done | bytes 331792 | tf_op jit(solution)/shard_map/reduce_scatter | solution.py:332
  1450.8 177.0 %all-reduce.8.cloned.1.call-done = bf16[1152,6,576]{2,0,1:T(8,128)(2,1)} async-done(((bf16[1152,6,576]{2,0,1:T(8,128)(2,1)}), bf16[1152,6,576]{2,0,1:T(8,128)(2,1)}) %all-reduce.8.cloned.1.call-update) | async-done | bytes 7962640
  1630.0 73.9 %reduce-scatter.31.cloned.1.call-done = bf16[72,1728]{1,0:T(8,128)(2,1)} async-done(((bf16[1152,1728]{1,0:T(8,128)(2,1)}), bf16[72,1728]{1,0:T(8,128)(2,1)}) %reduce-scatter.31.cloned.1.call-update) | async-done | bytes 248848
  (293 shorter events, 274.3 us)
Async XLA Ops:
  7.2 83.5 %all-gather.19.cloned.1.call-start = ((), (), s32[]{:S(2)}) async-start(), calls=%async_computation.9 | async-start | bytes 9400320 | tf_op jit(solution)/shard_map/all_gather | solution.py:68
  7.9 134.9 %all-gather.23.cloned.1.call-start = ((), (), s32[]{:S(2)}) async-start(), calls=%async_computation.11 | async-start | bytes 4700160 | tf_op jit(solution)/shard_map/all_gather | solution.py:69
  8.7 170.9 %all-gather.21.cloned.1.call-start = ((), (), s32[]{:S(2)}) async-start(), calls=%async_computation.10 | async-start | bytes 3538944 | tf_op jit(solution)/shard_map/all_gather | solution.py:77
  103.1 125.2 %all-gather.25.cloned.1.call-start = ((), (), s32[]{:S(2)}) async-start(), calls=%async_computation.12 | async-start | bytes 1566720 | tf_op jit(solution)/shard_map/all_gather | solution.py:71
  103.7 191.1 %reduce-scatter.17.cloned.1.call-start = ((), (), s32[]{:S(2)}) async-start(), calls=%async_computation.13 | async-start | bytes 7077888 | tf_op jit(solution)/shard_map/reduce_scatter | solution.py:206
  234.5 118.9 %all-gather.29.cloned.1.call-start = ((), (), s32[]{:S(2)}) async-start(), calls=%async_computation.15 | async-start | bytes 5640192 | tf_op jit(solution)/shard_map/all_gather | solution.py:70
  235.1 155.2 %all-gather.27.cloned.1.call-start = ((), (), s32[]{:S(2)}) async-start(), calls=%async_computation.14 | async-start | bytes 3538944 | tf_op jit(solution)/shard_map/all_gather | solution.py:81
  297.0 401.7 %copy-start.1 = (f32[512,1152]{1,0:T(8,128)}, f32[512,1152]{1,0:T(8,128)S(1)}, u32[]{:S(2)}) copy-start(f32[512,1152]{1,0:T(8,128)S(1)} %get-tuple-element.48) | copy-start | bytes 7077892
  299.4 149.6 %all-gather.31.cloned.1.call-start = ((), (), s32[]{:S(2)}) async-start(), calls=%async_computation.16 | async-start | bytes 5640192 | tf_op jit(solution)/shard_map/all_gather | solution.py:72
  300.2 195.8 %reduce-scatter.19.cloned.1.call-start = ((), (), s32[]{:S(2)}) async-start(), calls=%async_computation.17 | async-start | bytes 3538944 | tf_op jit(solution)/shard_map/reduce_scatter | solution.py:223
  462.5 74.1 %all-gather.33.cloned.1.call-start = ((), (), s32[]{:S(2)}) async-start(), calls=%async_computation.18 | async-start | bytes 3538944 | tf_op jit(solution)/shard_map/all_gather | solution.py:236
  500.4 94.8 %all-gather.35.cloned.1.call-start = ((), (), s32[]{:S(2)}) async-start(), calls=%async_computation.19 | async-start | bytes 5640192 | tf_op jit(solution)/shard_map/all_gather | solution.py:72
  536.7 115.5 %all-gather.37.cloned.1.call-start = ((), (), s32[]{:S(2)}) async-start(), calls=%async_computation.20 | async-start | bytes 5640192 | tf_op jit(solution)/shard_map/all_gather | solution.py:70
  537.2 159.2 %reduce-scatter.21.cloned.1.call-start = ((), (), s32[]{:S(2)}) async-start(), calls=%async_computation.21 | async-start | bytes 3538944 | tf_op jit(solution)/shard_map/reduce_scatter | solution.py:251
  663.0 75.0 %all-gather.41.cloned.1.call-start = ((), (), s32[]{:S(2)}) async-start(), calls=%async_computation.23 | async-start | bytes 1566720 | tf_op jit(solution)/shard_map/all_gather | solution.py:71
  663.6 110.8 %all-gather.39.cloned.1.call-start = ((), (), s32[]{:S(2)}) async-start(), calls=%async_computation.22 | async-start | bytes 3538944 | tf_op jit(solution)/shard_map/all_gather | solution.py:270
  702.7 167.1 %all-gather.43.cloned.1.call-start = ((), (), s32[]{:S(2)}) async-start(), calls=%async_computation.24 | async-start | bytes 4700160 | tf_op jit(solution)/shard_map/all_gather | solution.py:69
  704.2 210.1 %reduce-scatter.23.cloned.1.call-start = ((), (), s32[]{:S(2)}) async-start(), calls=%async_computation.25 | async-start | bytes 3538944 | tf_op jit(solution)/shard_map/reduce_scatter | solution.py:284
  879.9 66.6 %reduce-scatter.29.cloned.1.call-start = ((), (), s32[]{:S(2)}) async-start(), calls=%async_computation.32 | async-start | bytes 884736
  922.9 95.6 %all-gather.45.cloned.1.call-start = ((), (), s32[]{:S(2)}) async-start(), calls=%async_computation.26 | async-start | bytes 9400320 | tf_op jit(solution)/shard_map/all_gather | solution.py:68
  923.7 130.6 %all-gather.49.cloned.1.call-start = ((), (), s32[]{:S(2)}) async-start(), calls=%async_computation.29 | async-start | bytes 3538944 | tf_op jit(solution)/shard_map/all_gather | solution.py:81
  924.3 167.8 %all-gather.47.cloned.1.call-start = ((), (), s32[]{:S(2)}) async-start(), calls=%async_computation.28 | async-start | bytes 3538944 | tf_op jit(solution)/shard_map/all_gather | solution.py:77
  929.5 247.0 %reduce-scatter.27.cloned.1.call-start = ((), (), s32[]{:S(2)}) async-start(), calls=%async_computation.31 | async-start | bytes 5640192 | tf_op jit(solution)/shard_map/reduce_scatter | solution.py:338
  941.2 297.2 %reduce-scatter.33.cloned.1.call-start = ((), (), s32[]{:S(2)}) async-start(), calls=%async_computation.35 | async-start | bytes 1566720
  946.4 416.2 %all-reduce.6.cloned.1.call-start = ((), (), s32[]{:S(2)}) async-start(), calls=%async_computation.27 | async-start | bytes 147456 | tf_op jit(solution)/shard_map/psum | solution.py:352
  1025.3 423.7 %reduce-scatter.25.cloned.1.call-start = ((), (), s32[]{:S(2)}) async-start(), calls=%async_computation.30 | async-start | bytes 5640192 | tf_op jit(solution)/shard_map/reduce_scatter | solution.py:332
  1064.9 563.0 %all-reduce.8.cloned.1.call-start = ((), (), s32[]{:S(2)}) async-start(), calls=%async_computation.34 | async-start | bytes 17694720
  1072.3 631.5 %reduce-scatter.31.cloned.1.call-start = ((), (), s32[]{:S(2)}) async-start(), calls=%async_computation.33 | async-start | bytes 4386816
  1130.8 109.5 %copy-start.47 = (f32[1152]{0:T(1024)S(1)}, f32[1152]{0:T(1024)}, u32[]{:S(2)}) copy-start(f32[1152]{0:T(1024)} %get-tuple-element.71) | copy-start | bytes 13828
  1130.8 109.5 %copy-start.48 = (f32[1152]{0:T(1024)S(1)}, f32[1152]{0:T(1024)}, u32[]{:S(2)}) copy-start(f32[1152]{0:T(1024)} %get-tuple-element.75) | copy-start | bytes 13828
  1130.8 231.8 %copy-start.41 = (bf16[1,1152]{1,0:T(2,128)(2,1)S(1)}, bf16[1,1152]{1,0:T(2,128)(2,1)}, u32[]{:S(2)}) copy-start(bf16[1,1152]{1,0:T(2,128)(2,1)} %param.14) | copy-start | bytes 6916
  1130.8 231.8 %copy-start.43 = (f32[1,1152]{1,0:T(1,128)S(1)}, f32[1,1152]{1,0:T(1,128)}, u32[]{:S(2)}) copy-start(f32[1,1152]{1,0:T(1,128)} %copy-done.42) | copy-start | bytes 13828
  (58 other events, 780.1 us)
Sparse Core Ops, SparseCore 0:
  10.2 80.4 all-gather.18
  92.9 49.9 all-gather.22
  145.0 34.5 all-gather.20
  181.6 39.4 all-gather.24
  234.7 60.0 reduce-scatter.16
  297.0 56.3 all-gather.28
  355.6 34.6 all-gather.26
  392.7 56.3 all-gather.30
  462.7 33.2 reduce-scatter.18
  500.5 36.0 all-gather.32
  538.8 56.3 all-gather.34
  597.2 54.9 all-gather.36
  663.1 33.2 reduce-scatter.20
  698.6 39.3 all-gather.40
  739.5 34.8 all-gather.38
  776.7 51.7 all-gather.42
  880.0 34.3 reduce-scatter.22
  923.1 15.2 reduce-scatter.28
  940.8 77.7 all-gather.44
  1020.0 34.2 all-gather.48
  1056.0 36.0 all-gather.46
  1096.6 79.7 reduce-scatter.26
  1180.7 57.5 reduce-scatter.32
  1245.3 117.3 all-reduce.5
  1367.2 81.7 reduce-scatter.24
  1453.0 174.8 all-reduce.7
  1631.6 72.1 reduce-scatter.30
where the time goes:
time: 1720 us; the launch traced here: 1710 us
  waiting for transfers between devices  1280 us (74%)
  matrix products  221 us (13%)
  other arithmetic  95.6 us (6%)
  local copies, waits for them, and re-layouts  50.8 us (3%)
  blocking collectives  45.8 us (3%)
    unnamed x31, waiting for transfers between devices  315 us
    all_gather x2, waiting for transfers between devices, fetch_weights(): lax.all_gather(shards[0], 'fsdp', axis=0, tiled=True)  150 us
    all_gather x2, waiting for transfers between devices, fetch_weights(): lax.all_gather(shards[4], 'fsdp', axis=1, tiled=True)  105 us
    all_gather x2, waiting for transfers between devices, fetch_weights(): lax.all_gather(shards[2], 'fsdp', axis=0, tiled=True)  91.8 us
    reduce_scatter x1, waiting for transfers between devices, per_device(): lax.psum_scatter(up_grad.astype(jnp.bfloat16), 'fsdp', scatter_dimension=...  85 us
    psum x1, waiting for transfers between devices, per_device(): lax.psum((place_columns(qv_part, tensor_rank, tensor_size), place_columns...  78.9 us
    all_gather x2, waiting for transfers between devices, feed_gather(): return lax.all_gather(normed_low, 'tp', axis=0, tiled=True)  65.9 us
    reduce_scatter x1, waiting for transfers between devices, per_device(): lax.psum_scatter(jnp.dot(lax.slice_in_dim(heads_low, 0, local_rows * lax....  59 us
  transfers between devices with their start and end apart: 27, of which 24 were waited for; matrix products, arithmetic and copies ran while one was open for 18% of the time, Pallas kernels for 0%

commit v1 on v0

v1 whole, which is shorter than its diff:
```python
import functools
import math

import jax
import jax.numpy as jnp
from jax import lax
from jax.experimental import pallas as pl
from jax.experimental.pallas import tpu as pltpu
from jax.sharding import PartitionSpec as P

HD = 72


EPS = 1e-06
LOG2E = math.log2(math.e)
VMEM_LIMIT = 48 * 1024 * 1024
BOTH_LAST = (((1,), (1,)), ((), ()))
BOTH_FIRST = (((0,), (0,)), ((), ()))


def mm(a, b, dims=(((1,), (0,)), ((), ()))):
    return lax.dot_general(a, b, dims, preferred_element_type=jnp.float32)


def normalize(values):
    centred = values - jnp.mean(values, axis=-1, keepdims=True)
    inverse = lax.rsqrt(jnp.mean(centred * centred, axis=-1, keepdims=True) + EPS)
    return (centred * inverse, inverse)


def normalize_back(incoming, normed, inverse):
    first_mean = jnp.mean(incoming, axis=-1, keepdims=True)
    second_mean = jnp.mean(incoming * normed, axis=-1, keepdims=True)
    return inverse * (incoming - first_mean - normed * second_mean)


def modulate(normed, shift, scale):
    return (normed * (1.0 + scale) + shift).astype(jnp.bfloat16)


def silu_slope(values):
    sigmoid = jax.nn.sigmoid(values)
    return sigmoid * (1.0 + values * (1.0 - sigmoid))


def gelu_pair(values):
    root = math.sqrt(2.0 / math.pi)
    square = values * values
    bend = jnp.tanh(root * values * (1.0 + 0.044715 * square))
    half = 0.5 * (1.0 + bend)
    slope = half + 0.5 * values * (1.0 - bend * bend) * root * (1.0 + 3.0 * 0.044715 * square)
    return values * half, slope


def attend_kernel(start, packed_ref, out_ref, log_ref):
    rows, cols = out_ref.shape
    factor = LOG2E / math.sqrt(HD)
    pieces = []
    for head in range(cols // HD):
        at = head * HD
        queries = packed_ref[start : start + rows, at : at + HD]
        key_rows = packed_ref[:, cols + at : cols + at + HD]
        value_rows = packed_ref[:, 2 * cols + at : 2 * cols + at + HD]
        scores = mm(key_rows, queries, BOTH_LAST)
        top = jnp.max(scores, axis=0, keepdims=True)
        shares = jnp.exp2((scores - top) * factor)
        total = jnp.sum(shares, axis=0, keepdims=True)
        piece = mm(value_rows, shares.astype(jnp.bfloat16), BOTH_FIRST)
        pieces.append(piece / total)
        log_ref[head : head + 1, :] = top * factor + jnp.log2(total)
    out_ref[...] = jnp.concatenate(pieces, axis=0).T.astype(jnp.bfloat16)


def attend(packed, start, rows):
    length, width = packed.shape
    cols = width // 3
    heads = cols // HD
    return pl.pallas_call(
        functools.partial(attend_kernel, start),
        out_shape=(
            jax.ShapeDtypeStruct((rows, cols), jnp.bfloat16),
            jax.ShapeDtypeStruct((heads, rows), jnp.float32),
        ),
        in_specs=[pl.BlockSpec(memory_space=pltpu.VMEM)],
        out_specs=(pl.BlockSpec(memory_space=pltpu.VMEM),) * 2,
        compiler_params=pltpu.CompilerParams(vmem_limit_bytes=VMEM_LIMIT),
        cost_estimate=pl.CostEstimate(
            flops=4 * rows * length * 256 * heads,
            bytes_accessed=packed.size * 2 + rows * cols * 2,
            transcendentals=rows * length * heads,
        ),
    )(packed)


def attend_back_kernel(start, last, *refs):
    if last:
        packed_ref, up_ref, heads_ref, log_ref, key_in, value_in, query_ref, key_ref, value_ref = refs
    else:
        packed_ref, up_ref, heads_ref, log_ref, query_ref, key_ref, value_ref = refs
    rows, cols = up_ref.shape
    scale = 1.0 / math.sqrt(HD)
    factor = LOG2E * scale
    products = (up_ref[...].astype(jnp.float32) * heads_ref[...].astype(jnp.float32)).T
    pieces = []
    for head in range(cols // HD):
        at = head * HD
        here = slice(at, at + HD)
        queries = packed_ref[start : start + rows, at : at + HD]
        key_rows = packed_ref[:, cols + at : cols + at + HD]
        value_rows = packed_ref[:, 2 * cols + at : 2 * cols + at + HD]
        incoming = up_ref[:, here]
        inner = jnp.sum(products[here], axis=0, keepdims=True)
        scores = mm(key_rows, queries, BOTH_LAST)
        shares = jnp.exp2(scores * factor - log_ref[head : head + 1, :])
        grads = mm(value_rows, incoming, BOTH_LAST)
        score_grads = (shares * (grads - inner)).astype(jnp.bfloat16)
        value_grad = jnp.dot(shares.astype(jnp.bfloat16), incoming, preferred_element_type=jnp.float32)
        key_grad = jnp.dot(score_grads, queries, preferred_element_type=jnp.float32) * scale
        if last:
            value_grad += value_in[:, here]
            key_grad += key_in[:, here]
        value_ref[:, here] = value_grad.astype(value_ref.dtype)
        key_ref[:, here] = key_grad.astype(key_ref.dtype)
        pieces.append(mm(key_rows, score_grads, BOTH_FIRST) * scale)
    query_ref[...] = jnp.concatenate(pieces, axis=0).T.astype(jnp.bfloat16)


def attend_back(packed, start, upstream, heads_low, logs, sums, last):
    length, width = packed.shape
    cols = width // 3
    heads = cols // HD
    rows = upstream.shape[0]
    kind = jnp.bfloat16 if last else jnp.float32
    operands = (packed, upstream, heads_low, logs) + (sums if last else ())
    return pl.pallas_call(
        functools.partial(attend_back_kernel, start, last),
        out_shape=(
            jax.ShapeDtypeStruct((rows, cols), jnp.bfloat16),
            jax.ShapeDtypeStruct((length, cols), kind),
            jax.ShapeDtypeStruct((length, cols), kind),
        ),
        in_specs=[pl.BlockSpec(memory_space=pltpu.VMEM)] * len(operands),
        out_specs=(pl.BlockSpec(memory_space=pltpu.VMEM),) * 3,
        compiler_params=pltpu.CompilerParams(vmem_limit_bytes=VMEM_LIMIT),
        cost_estimate=pl.CostEstimate(
            flops=10 * rows * length * 256 * heads,
            bytes_accessed=packed.size * 2 + rows * cols * 6 + length * cols * 8,
            transcendentals=rows * length * heads,
        ),
    )(*operands)


def swap(values):
    return lax.ppermute(values, "tp", [(0, 1), (1, 0)])


def gather_rows(own, paired):
    if paired:
        return [own, swap(own)]
    return [lax.all_gather(own, "tp", axis=0, tiled=True)]


def scatter_rows(parts, paired):
    if paired:
        return parts[0] + swap(parts[1].astype(jnp.bfloat16)).astype(jnp.float32)
    whole = jnp.concatenate(parts, axis=0).astype(jnp.bfloat16)
    return lax.psum_scatter(whole, "tp", scatter_dimension=0, tiled=True).astype(jnp.float32)


def gather_columns(own):
    if lax.axis_size("tp") == 2:
        other = swap(own)
        left = lax.axis_index("tp") == 0
        return jnp.concatenate([jnp.where(left, own, other), jnp.where(left, other, own)], axis=-1)
    return lax.all_gather(own, "tp", axis=own.ndim - 1, tiled=True)


def scatter_columns(whole):
    count = lax.axis_size("tp")
    if count == 2:
        width = whole.shape[-1] // 2
        left = lax.axis_index("tp") == 0
        halves = whole[..., :width], whole[..., width:]
        own = jnp.where(left, halves[0], halves[1])
        return own + swap(jnp.where(left, halves[1], halves[0]))
    return lax.psum_scatter(whole, "tp", scatter_dimension=whole.ndim - 1, tiled=True)


def sum_pair(values):
    if lax.axis_size("tp") == 2:
        return values + swap(values)
    return lax.psum(values, "tp")


def exchange(blocks):
    return lax.all_to_all(blocks, "fsdp", 0, 0, tiled=True)


def share(values):
    return exchange(jnp.broadcast_to(values[None], (lax.axis_size("fsdp"),) + values.shape))


def per_device(
    inputs,
    conditions,
    modulation_weight,
    modulation_bias,
    attention_weight,
    attention_bias,
    output_weight,
    output_bias,
    up_weight,
    up_bias,
    down_weight,
    down_bias,
    cotangent,
):
    tp = lax.axis_size("tp")
    rank = lax.axis_index("tp")
    fsdp = lax.axis_size("fsdp")
    local_rows, width = inputs.shape
    latents = conditions.shape[0]
    length = local_rows * tp // latents
    depth = attention_weight.shape[0]
    cols = attention_weight.shape[2]
    hidden = up_weight.shape[1]
    paired = tp == 2 and latents == 1
    f32 = jnp.float32
    bf16 = jnp.bfloat16

    first_shard = jnp.concatenate([attention_weight.reshape(depth, 3 * cols), output_weight.T], axis=1)
    first_weights = lax.all_gather(first_shard, "fsdp", axis=0, tiled=True)
    up_all = lax.all_gather(up_weight, "fsdp", axis=0, tiled=True)
    down_all = lax.all_gather(down_weight.T, "fsdp", axis=0, tiled=True)
    attention_all = first_weights[:, : 3 * cols]
    output_all = first_weights[:, 3 * cols :]

    condition_values = conditions.astype(f32)
    silu_low = jax.nn.silu(condition_values).astype(bf16)
    silu_rows = exchange(silu_low.reshape(latents, fsdp, depth).transpose(1, 0, 2))
    silu_rows = silu_rows.reshape(fsdp * latents, depth)
    modulation_flat = modulation_weight.reshape(depth, 6 * cols)
    partial = mm(silu_rows, modulation_flat).reshape(fsdp, latents, 6 * cols)
    own_columns = jnp.sum(exchange(partial), axis=0).reshape(latents, 6, cols)
    modulation = gather_columns(own_columns + modulation_bias.astype(f32))
    own_modulation = modulation[0]
    if latents > 1:
        own_modulation = lax.dynamic_index_in_dim(
            modulation, rank * local_rows // length, 0, keepdims=False
        )

    def own_rows(group):
        return own_modulation[group][None]

    def all_rows(group):
        if latents == 1:
            return modulation[0, group][None]
        return jnp.repeat(modulation[:, group], length, axis=0)

    def sum_latents(values):
        return jnp.sum(values.reshape(latents, length, width), axis=1)

    def place_latent(values):
        total = jnp.sum(values, axis=0)[None]
        if latents == 1:
            return total
        mine = jnp.arange(latents)[:, None] == rank * local_rows // length
        return jnp.where(mine, total, 0.0)

    inputs_all = jnp.concatenate(gather_rows(inputs, paired), axis=0)
    cotangent_parts = gather_rows(cotangent, paired)
    input_values = inputs.astype(f32)
    first_normed, first_inverse = normalize(input_values)
    first_normed_all, _ = normalize(inputs_all.astype(f32))
    first_all = modulate(first_normed_all, all_rows(0), all_rows(1))
    bias_rows = attention_bias.astype(f32)
    packed_bias = jnp.concatenate([bias_rows[0], jnp.zeros((cols,), f32), bias_rows[1]])
    packed = (mm(first_all, attention_all) + packed_bias).astype(bf16)

    block = local_rows
    blocks = length // block
    group_blocks = latents * blocks
    packed_latents = [packed[n * length : (n + 1) * length] for n in range(latents)]
    heads_parts = [None] * group_blocks
    logs = [None] * group_blocks
    products = [None] * group_blocks
    for at in reversed(range(group_blocks)):
        latent, start = at // blocks, at % blocks * block
        heads_parts[at], logs[at] = attend(packed_latents[latent], start, block)
        products[at] = mm(heads_parts[at], output_all, BOTH_LAST)
    attention = scatter_rows(products, paired) + output_bias.astype(f32)
    mid = input_values + own_rows(2) * attention
    second_normed, second_inverse = normalize(mid)
    second_parts = gather_rows(modulate(second_normed, own_rows(3), own_rows(4)), paired)

    gate_all = all_rows(5)
    if paired:
        feed_parts = [(gate_all * part.astype(f32)).astype(bf16) for part in cotangent_parts]
    else:
        feed_parts = [(gate_all * cotangent_parts[0].astype(f32)).astype(bf16)]
    up_bias_row = up_bias.astype(f32)[None]
    act_parts = []
    pre_parts = []
    for second, feed_grad in zip(second_parts, feed_parts):
        act, slope = gelu_pair(mm(second, up_all) + up_bias_row)
        act_parts.append(act.astype(bf16))
        pre_parts.append((mm(feed_grad, down_all) * slope).astype(bf16))
    second_grad = scatter_rows([mm(part, up_all, BOTH_LAST) for part in pre_parts], paired)
    feed = scatter_rows([mm(part, down_all, BOTH_LAST) for part in act_parts], paired)
    feed = feed + down_bias.astype(f32)
    outputs = (mid + own_rows(5) * feed).astype(bf16)

    feed_all = jnp.concatenate(feed_parts, axis=0)
    act_all = jnp.concatenate(act_parts, axis=0)
    pre_all = jnp.concatenate(pre_parts, axis=0)
    second_all = jnp.concatenate(second_parts, axis=0)

    def scatter_weights(values):
        return lax.psum_scatter(
            values.astype(bf16), "fsdp", scatter_dimension=0, tiled=True
        ).astype(f32)

    grad_down = scatter_weights(mm(feed_all, act_all, BOTH_FIRST))
    grad_up_weight = scatter_weights(mm(second_all, pre_all, BOTH_FIRST))

    upstream = cotangent.astype(f32)
    mid_grad = upstream + normalize_back(
        second_grad * (1.0 + own_rows(4)), second_normed, second_inverse
    )
    attention_low = (own_rows(2) * mid_grad).astype(bf16)
    upstream_parts = gather_rows(attention_low, paired)
    if paired:
        heads_grads = [mm(part, output_all).astype(bf16) for part in upstream_parts]
    else:
        heads_grad = mm(upstream_parts[0], output_all).astype(bf16)
        heads_grads = [heads_grad[n * block : (n + 1) * block] for n in range(group_blocks)]
    query_grads = []
    key_grads = []
    value_grads = []
    for latent in range(latents):
        sums = ()
        for step in range(blocks):
            at = latent * blocks + step
            query_grad, *sums = attend_back(
                packed_latents[latent],
                step * block,
                heads_grads[at],
                heads_parts[at],
                logs[at],
                tuple(sums),
                step == blocks - 1,
            )
            query_grads.append(query_grad)
        key_grads.append(sums[0])
        value_grads.append(sums[1])
    packed_low = jnp.concatenate(
        [jnp.concatenate(part, axis=0) for part in (query_grads, key_grads, value_grads)], axis=1
    )
    first_grad_all = mm(packed_low, attention_all, BOTH_LAST)
    attention_grad = mm(first_all, packed_low, BOTH_FIRST)
    output_grad = mm(
        jnp.concatenate(upstream_parts, axis=0), jnp.concatenate(heads_parts, axis=0), BOTH_FIRST
    )
    first_grads = scatter_weights(jnp.concatenate([attention_grad, output_grad], axis=1))

    if paired:
        first_grad_parts = [first_grad_all[:local_rows], first_grad_all[local_rows:]]
    else:
        first_grad_parts = [first_grad_all]
    first_grad = scatter_rows(first_grad_parts, paired)
    grad_inputs = mid_grad + normalize_back(
        first_grad * (1.0 + own_rows(1)), first_normed, first_inverse
    )

    modulation_parts = jnp.stack(
        [
            sum_latents(first_grad_all),
            sum_latents(first_grad_all * first_normed_all),
            place_latent(mid_grad * attention),
            place_latent(second_grad),
            place_latent(second_grad * second_normed),
            place_latent(upstream * feed),
        ],
        axis=1,
    )
    modulation_low = scatter_columns(modulation_parts).astype(bf16)
    modulation_all = share(modulation_low.reshape(latents, 6 * cols)).reshape(
        fsdp * latents, 6 * cols
    )
    grad_modulation_weight = mm(silu_rows, modulation_all, BOTH_FIRST).reshape(depth, 6, cols)
    grad_modulation_bias = jnp.sum(modulation_all, axis=0, dtype=f32).reshape(6, cols)
    silu_part = sum_pair(mm(modulation_all, modulation_flat, BOTH_LAST))
    silu_total = exchange(silu_part.reshape(fsdp, latents, depth))
    silu_total = silu_total.transpose(1, 0, 2).reshape(latents, width)
    grad_conditions = silu_total * silu_slope(condition_values)

    own_feed = feed_parts[0]
    if not paired:
        own_feed = (own_rows(5) * upstream).astype(bf16)
    token_sums = sum_pair(
        jnp.concatenate(
            [
                jnp.sum(attention_low, axis=0, dtype=f32),
                jnp.sum(own_feed, axis=0, dtype=f32),
            ]
        )
    )
    bias_parts = jnp.concatenate(
        [
            token_sums,
            jnp.sum(packed_low, axis=0, dtype=f32),
            jnp.sum(pre_all, axis=0, dtype=f32),
        ]
    )
    bias_sums = jnp.sum(share(bias_parts), axis=0)
    grad_output_bias = bias_sums[:width]
    grad_down_bias = bias_sums[width : 2 * width]
    packed_sums = bias_sums[2 * width : 2 * width + 3 * cols]
    grad_attention_bias = jnp.stack([packed_sums[:cols], packed_sums[2 * cols :]])
    grad_up_bias = bias_sums[2 * width + 3 * cols :]
    return (
        outputs,
        grad_inputs,
        grad_conditions,
        grad_modulation_weight,
        grad_modulation_bias,
        first_grads[:, : 3 * cols].reshape(depth, 3, cols),
        grad_attention_bias,
        first_grads[:, 3 * cols :].T,
        grad_output_bias,
        grad_up_weight,
        grad_up_bias,
        grad_down.T,
        grad_down_bias,
    )


def solution(mesh):
    placed = (
        P(("fsdp", "tp"), None),
        P("fsdp", None),
        P("fsdp", None, "tp"),
        P(None, "tp"),
        P("fsdp", None, "tp"),
        P(None, "tp"),
        P("tp", "fsdp"),
        P(),
        P("fsdp", "tp"),
        P("tp"),
        P("tp", "fsdp"),
        P(),
        P(("fsdp", "tp"), None),
    )
    return jax.shard_map(
        per_device,
        mesh=mesh,
        in_specs=placed,
        out_specs=(
            P(("fsdp", "tp"), None),
            P(("fsdp", "tp"), None),
            P("fsdp", None),
            P("fsdp", None, "tp"),
            P(None, "tp"),
            P("fsdp", None, "tp"),
            P(None, "tp"),
            P("tp", "fsdp"),
            P(),
            P("fsdp", "tp"),
            P("tp"),
            P("tp", "fsdp"),
            P(),
        ),
        check_vma=False,
    )
```

time: 1720 us -> 478 us (0.28)
  waiting for transfers between devices: 1280 us -> 188 us
  matrix products: 221 us -> 116 us
  other arithmetic: 95.6 us -> 31.7 us
  blocking collectives: 45.8 us -> 0 us
  Pallas kernels: 0 us -> 45.4 us
  starting transfers between devices: 1.9 us -> 35.8 us
    all_gather x16 -> x3, waiting for transfers between devices: 613 us -> 55.5 us  [the longest x1 47.5 us: per_device(): down_all = lax.all_gather(down_weight.T, 'fsdp', axis=0, tiled=True)]
    unnamed x31 -> x7, waiting for transfers between devices: 315 us -> 8.85 us
    reduce_scatter x6 -> x2, waiting for transfers between devices: 275 us -> 0.01 us  [scatter_weights(): lax.psum_scatter(values.astype(bf16), 'fsdp', scatter_dimension=0, tiled=...]
    dot_general x32 -> x21, matrix products: 221 us -> 116 us  [mm(): return lax.dot_general(a, b, dims, preferred_element_type=jnp.float32)]
    ppermute x0 -> x12, waiting for transfers between devices: none -> 86.1 us  [swap(): return lax.ppermute(values, 'tp', [(0, 1), (1, 0)])]
    psum x1 -> x0, waiting for transfers between devices: 78.9 us -> none  [per_device(): lax.psum((place_columns(qv_part, tensor_rank, tensor_size), place_columns...]
    pallas_call x0 -> x4, Pallas kernels: none -> 45.4 us  [the longest x2 29.1 us: attend_back(): pl.pallas_call(functools.partial(attend_back_kernel, start, last), out_sh...]
    convert_element_type x13 -> x8, other arithmetic: 46 us -> 2.64 us  [the longest x2 1.94 us: scatter_weights(): return lax.psum_scatter(values.astype(bf16), 'fsdp', scatter_dimension=0,...]
  transfers between devices with their start and end apart: 27 -> 23, of which waited for: 24 -> 17; matrix products, arithmetic and copies ran while one was open for 18% -> 33% of each run, Pallas kernels for 0% -> 10%
where the time goes in v1:
time: 478 us; the launch traced here: 472 us
  waiting for transfers between devices  188 us (39%)
  matrix products  116 us (24%)
  Pallas kernels  45.4 us (9%)
  local copies, waits for them, and re-layouts  39.4 us (8%)
  starting transfers between devices  35.8 us (7%)
  other arithmetic  31.7 us (7%)
  between operations  15.5 us (3%)
    dot_general x21, matrix products, mm(): return lax.dot_general(a, b, dims, preferred_element_type=jnp.float32)  116 us
    ppermute x12, waiting for transfers between devices, swap(): return lax.ppermute(values, 'tp', [(0, 1), (1, 0)])  86.1 us
    all_gather x1, waiting for transfers between devices, per_device(): down_all = lax.all_gather(down_weight.T, 'fsdp', axis=0, tiled=True)  47.5 us
    all_to_all x5, waiting for transfers between devices, exchange(): return lax.all_to_all(blocks, 'fsdp', 0, 0, tiled=True)  37.8 us
    pallas_call x2, Pallas kernels, attend_back(): pl.pallas_call(functools.partial(attend_back_kernel, start, last), out_sh...  29.1 us
    all_to_all x5, starting transfers between devices, exchange(): return lax.all_to_all(blocks, 'fsdp', 0, 0, tiled=True)  21.2 us
    unnamed x103, local copies, waits for them, and re-layouts  20.4 us
    pallas_call x2, Pallas kernels, attend(): pl.pallas_call(functools.partial(attend_kernel, start), out_shape=(jax.Sh...  16.3 us
  transfers between devices with their start and end apart: 23, of which 17 were waited for; matrix products, arithmetic and copies ran while one was open for 33% of the time, Pallas kernels for 10%

profile of v1, /device:TPU:0, one launch (start us, length us, event | category | flops | bytes accessed | tf_op | source)
XLA Modules:
  0.0 471.8 jit_solution(834889356648312502)
XLA Ops:
  16.3 5.9 %all-to-all-start = ((bf16[16,1,72]{2,1,0:T(2,128)(2,1)}), bf16[16,1,72]{2,1,0:T(2,128)(2,1)S(1)}, u32[]{:S(2)}, u32[]{:S(2)}) async-start(bf16[16,1,72]{2,1,0:T(2,128)(2,1)} %transpose_reshape.4), calls=%async_computation | async-start | bytes 16384 | tf_op jit(solution)/shard_map/all_to_all | solution.py:196
  33.9 8.6 %all-to-all-done.1 = f32[16,1,3456]{2,1,0:T(1,128)S(1)} async-done(((f32[16,1,3456]{2,1,0:T(1,128)}), f32[16,1,3456]{2,1,0:T(1,128)S(1)}, u32[]{:S(2)}, u32[]{:S(2)}) %all-to-all-start.1) | async-done | bytes 221216 | tf_op jit(solution)/shard_map/all_to_all | solution.py:196
  43.8 22.9 %collective-permute-done = f32[1,6,576]{2,1,0:T(8,128)S(1)} collective-permute-done((f32[1,6,576]{2,1,0:T(8,128)S(1)}, f32[1,6,576]{2,1,0:T(8,128)S(1)}, u32[]{:S(2)}, u32[]{:S(2)}) %collective-permute-start) | collective-permute-done | bytes 13856 | tf_op jit(solution)/shard_map/ppermute | solution.py:154
  71.7 8.9 %add_convert_fusion.packed_ref.refs_0_ = bf16[1024,1728]{1,0:T(8,128)(2,1)S(1)} fusion(f32[1728]{0:T(1024)S(1)} %concatenate.49, bf16[1152,2304]{1,0:T(8,128)(2,1)} %all-gather.4.cloned.1.call-done, f32[1152]{0:T(1024)S(1)} %get-tuple-element.134, f32[1152]{0:T(1024)S(1)} %get-tuple-element.135, f32[1024]{0:T(1024)S(1)} %add_rsqrt_fusion, ...), kind=kOutput, calls=%fused_computation.5 | convolution fusion | flops 4091019264 | bytes 10051328 | tf_op jit(solution)/shard_map/dot_general | solution.py:22
  80.7 8.0 %shard_map.229 = (bf16[512,576]{1,0:T(8,128)(2,1)S(1)}, f32[8,512]{1,0:T(8,128)S(1)}) custom-call(bf16[1024,1728]{1,0:T(8,128)(2,1)S(1)} %add_convert_fusion.packed_ref.refs_0_), custom_call_target="tpu_custom_call" | custom-call | flops 4294967296 | bytes 4128768 | tf_op jit(solution)/shard_map/pallas_call | solution.py:78
  95.0 8.3 %shard_map.228 = (bf16[512,576]{1,0:T(8,128)(2,1)S(1)}, f32[8,512]{1,0:T(8,128)S(1)}) custom-call(bf16[1024,1728]{1,0:T(8,128)(2,1)S(1)} %add_convert_fusion.packed_ref.refs_0_), custom_call_target="tpu_custom_call" | custom-call | flops 4294967296 | bytes 4128768 | tf_op jit(solution)/shard_map/pallas_call | solution.py:78
  103.4 14.8 %collective-permute-done.2 = bf16[512,1152]{1,0:T(8,128)(2,1)S(1)} collective-permute-done((bf16[512,1152]{1,0:T(8,128)(2,1)S(1)}, bf16[512,1152]{1,0:T(8,128)(2,1)S(1)}, u32[]{:S(2)}, u32[]{:S(2)}) %collective-permute-start.2) | collective-permute-done | bytes 1179680 | tf_op jit(solution)/shard_map/ppermute | solution.py:154
  128.9 9.8 %multiply_convert_fusion.1 = (bf16[512,2304]{1,0:T(8,128)(2,1)}, f32[512,2304]{1,0:T(8,128)}) fusion(f32[2304]{0:T(1024)S(1)} %convert_element_type.139, bf16[512,1152]{1,0:T(8,128)(2,1)} %add_convert_fusion.2, bf16[1152,2304]{1,0:T(8,128)(2,1)} %all-gather.6.cloned.1.call-done), kind=kOutput, calls=%fused_computation.28 | convolution fusion | flops 2729705472 | bytes 13575168 | tf_op jit(solution)/shard_map/dot_general | solution.py:22
  138.6 47.5 %all-gather.8.cloned.1.call-done = bf16[1152,2304]{1,0:T(8,128)(2,1)} async-done(((bf16[72,2304]{1,0:T(8,128)(2,1)}), bf16[1152,2304]{1,0:T(8,128)(2,1)}) %all-gather.8.cloned.1.call-update) | async-done | bytes 5308432 | tf_op jit(solution)/shard_map/all_gather | solution.py:234
  186.2 8.1 %fusion.11 = bf16[512,2304]{1,0:T(8,128)(2,1)S(1)} fusion(f32[512,2304]{1,0:T(8,128)} %get-tuple-element.166, bf16[512,1152]{1,0:T(8,128)(2,1)S(1)} %copy-done.25, bf16[1152,2304]{1,0:T(8,128)(2,1)} %all-gather.8.cloned.1.call-done), kind=kOutput, calls=%fused_computation.31 | convolution fusion | flops 2739142656 | bytes 13565952 | tf_op jit(solution)/shard_map/dot_general | solution.py:22
  194.4 7.6 %multiply_convert_fusion = (bf16[512,2304]{1,0:T(8,128)(2,1)}, f32[512,2304]{1,0:T(8,128)S(1)}) fusion(f32[2304]{0:T(1024)S(1)} %convert_element_type.139, bf16[512,1152]{1,0:T(8,128)(2,1)} %collective-permute-done.3, bf16[1152,2304]{1,0:T(8,128)(2,1)S(1)} %copy-done.41), kind=kOutput, calls=%fused_computation.25 | convolution fusion | flops 2729705472 | bytes 13575168 | tf_op jit(solution)/shard_map/dot_general | solution.py:22
  201.9 4.8 %fusion.12 = bf16[512,2304]{1,0:T(8,128)(2,1)S(1)} fusion(f32[512,2304]{1,0:T(8,128)S(1)} %get-tuple-element.168, bf16[512,1152]{1,0:T(8,128)(2,1)S(1)} %copy-done.26, bf16[1152,2304]{1,0:T(8,128)(2,1)S(1)} %copy-done.40), kind=kOutput, calls=%fused_computation.32 | convolution fusion | flops 2739142656 | bytes 13565952 | tf_op jit(solution)/shard_map/dot_general | solution.py:22
  208.2 9.2 %convolution_convert_fusion.1 = bf16[1152,2304]{1,0:T(8,128)(2,1)} fusion(bf16[512,2304]{1,0:T(8,128)(2,1)S(1)} %fusion.12, bf16[512,2304]{1,0:T(8,128)(2,1)S(1)} %fusion.11, bf16[512,1152]{1,0:T(8,128)(2,1)} %collective-permute-done.3, bf16[512,1152]{1,0:T(8,128)(2,1)} %add_convert_fusion.2), kind=kOutput, calls=%fused_computation.1 | convolution fusion | flops 5452627968 | bytes 12386304 | tf_op jit(solution)/shard_map/dot_general | solution.py:22
  217.5 7.6 %convolution_convert_fusion.4 = bf16[512,1152]{1,0:T(8,128)(2,1)} fusion(bf16[512,2304]{1,0:T(8,128)(2,1)} %copy-done.21, bf16[1152,2304]{1,0:T(8,128)(2,1)} %all-gather.6.cloned.1.call-done), kind=kOutput, calls=%fused_computation.44 | convolution fusion | flops 2718498816 | bytes 8847360 | tf_op jit(solution)/shard_map/dot_general | solution.py:22
  226.6 7.7 %convolution_convert_fusion = bf16[1152,2304]{1,0:T(8,128)(2,1)} fusion(bf16[512,2304]{1,0:T(8,128)(2,1)S(1)} %copy-done.44, bf16[512,2304]{1,0:T(8,128)(2,1)S(1)} %copy-done.42, bf16[512,1152]{1,0:T(8,128)(2,1)S(1)} %copy-done.27, bf16[512,1152]{1,0:T(8,128)(2,1)S(1)} %copy-done.25), kind=kOutput, calls=%fused_computation | convolution fusion | flops 5452627968 | bytes 12386304 | tf_op jit(solution)/shard_map/dot_general | solution.py:22
  234.5 6.9 %convolution_convert_fusion.5 = bf16[512,1152]{1,0:T(8,128)(2,1)S(1)} fusion(bf16[512,2304]{1,0:T(8,128)(2,1)} %get-tuple-element.167, bf16[1152,2304]{1,0:T(8,128)(2,1)} %all-gather.8.cloned.1.call-done), kind=kOutput, calls=%fused_computation.45 | convolution fusion | flops 2718498816 | bytes 8847360 | tf_op jit(solution)/shard_map/dot_general | solution.py:22
  242.1 12.1 %collective-permute-done.6 = bf16[512,1152]{1,0:T(8,128)(2,1)} collective-permute-done((bf16[512,1152]{1,0:T(8,128)(2,1)}, bf16[512,1152]{1,0:T(8,128)(2,1)}, u32[]{:S(2)}, u32[]{:S(2)}) %collective-permute-start.6) | collective-permute-done | bytes 1179680 | tf_op jit(solution)/shard_map/ppermute | solution.py:154
  254.3 6.7 %multiply_reduce_fusion = (f32[1152]{0:T(1024)S(1)}, f32[512]{0:T(512)S(1)}, f32[512]{0:T(512)S(1)}, f32[1152]{0:T(1024)S(1)}, f32[512,1152]{1,0:T(8,128)S(1)}) fusion(f32[512,1152]{1,0:T(8,128)S(1)} %copy-done.12, f32[512]{0:T(512)S(1)} %add_rsqrt_fusion.2, f32[512]{0:T(512)S(1)} %broadcast_multiply_fusion.6, ...), kind=kOutput, calls=%fused_computation.73 | convolution fusion | flops 2724393984 | bytes 13587968 | tf_op jit(solution)/shard_map/dot_general | solution.py:22
  261.0 17.8 %collective-permute-done.4 = bf16[512,1152]{1,0:T(8,128)(2,1)S(1)} collective-permute-done((bf16[512,1152]{1,0:T(8,128)(2,1)S(1)}, bf16[512,1152]{1,0:T(8,128)(2,1)S(1)}, u32[]{:S(2)}, u32[]{:S(2)}) %collective-permute-start.4) | collective-permute-done | bytes 1179680 | tf_op jit(solution)/shard_map/ppermute | solution.py:154
  278.8 7.5 %fusion.26 = (f32[1152]{0:T(1024)S(1)}, bf16[512,1152]{1,0:T(8,128)(2,1)}, f32[1152]{0:T(1024)S(1)}, bf16[512,1152]{1,0:T(8,128)(2,1)}, f32[512,1152]{1,0:T(8,128)}) fusion(bf16[512,1152]{1,0:T(8,128)(2,1)S(1)} %copy-done.24, bf16[512,1152]{1,0:T(8,128)(2,1)S(1)} %collective-permute-done.4, f32[1152]{0:T(1024)S(1)} %convert_element_type.144, ...), kind=kOutput, calls=%fused_computation.57 | convolution fusion | flops 2731472896 | bytes 20679680 | tf_op jit(solution)/shard_map/dot_general | solution.py:22
  291.4 14.3 %shard_map.230 = (bf16[512,576]{1,0:T(8,128)(2,1)S(1)}, f32[1024,576]{1,0:T(8,128)S(1)}, f32[1024,576]{1,0:T(8,128)}) custom-call(bf16[1024,1728]{1,0:T(8,128)(2,1)} %copy-done.5, bf16[512,576]{1,0:T(8,128)(2,1)S(1)} %copy.88.refs_1_, bf16[512,576]{1,0:T(8,128)(2,1)S(1)} %get-tuple-element.23.refs_2_, f32[8,512]{1,0:T(8,128)S(1)} %get-tuple-element.25.refs_3_), custom_call_target="tpu_custom_call" | custom-call | flops 10737418240 | bytes 10027008 | tf_op jit(solution)/shard_map/pallas_call | solution.py:135
  307.2 6.8 %collective-permute-done.7 = bf16[512,1152]{1,0:T(8,128)(2,1)} collective-permute-done((bf16[512,1152]{1,0:T(8,128)(2,1)}, bf16[512,1152]{1,0:T(8,128)(2,1)}, u32[]{:S(2)}, u32[]{:S(2)}) %collective-permute-start.7) | collective-permute-done | bytes 1179680 | tf_op jit(solution)/shard_map/ppermute | solution.py:154
  320.7 14.8 %shard_map.231 = (bf16[512,576]{1,0:T(8,128)(2,1)S(1)}, bf16[1024,576]{1,0:T(8,128)(2,1)S(1)}, bf16[1024,576]{1,0:T(8,128)(2,1)S(1)}) custom-call(bf16[1024,1728]{1,0:T(8,128)(2,1)} %copy-done.5, bf16[512,576]{1,0:T(8,128)(2,1)S(1)} %copy-done, bf16[512,576]{1,0:T(8,128)(2,1)S(1)} %copy-done.4, f32[8,512]{1,0:T(8,128)S(1)} %get-tuple-element.27.refs_3_, ...), custom_call_target="tpu_custom_call" | custom-call | flops 10737418240 | bytes 10027008 | tf_op jit(solution)/shard_map/pallas_call | solution.py:135
  336.7 6.4 %concatenate.51 = bf16[1024,1728]{1,0:T(8,128)(2,1)} concatenate(bf16[1024,576]{1,0:T(8,128)(2,1)} %pad_maximum_fusion.4, bf16[1024,576]{1,0:T(8,128)(2,1)S(1)} %get-tuple-element.31, bf16[1024,576]{1,0:T(8,128)(2,1)S(1)} %get-tuple-element.32), dimensions={1} | concatenate | bytes 7077888 | tf_op jit(solution)/shard_map/concatenate | solution.py:356
  346.8 5.0 %convolution_convert_fusion.2 = bf16[1152,1728]{0,1:T(8,128)(2,1)S(1)} fusion(bf16[1024,1728]{1,0:T(8,128)(2,1)S(1)} %copy-done.9, f32[1152]{0:T(1024)S(1)} %get-tuple-element.134, f32[1152]{0:T(1024)S(1)} %get-tuple-element.135, f32[1024]{0:T(1024)S(1)} %add_rsqrt_fusion, f32[1024]{0:T(1024)S(1)} %broadcast_multiply_fusion, ...), kind=kOutput, calls=%fused_computation.3 | convolution fusion | flops 4089470976 | bytes 9896960 | tf_op jit(solution)/shard_map/dot_general | solution.py:22
  354.6 8.8 %copy.96 = bf16[1152,2304]{1,0:T(8,128)(2,1)} copy(bf16[1152,2304]{0,1:T(8,128)(2,1)} %pad_maximum_fusion) | data formatting | bytes 10616832
  368.1 9.4 %fusion.6 = (f32[1152]{0:T(1024)S(1)}, f32[1152]{0:T(1024)S(1)}, f32[1024,1152]{1,0:T(8,128)}) fusion(f32[1024]{0:T(1024)S(1)} %add_rsqrt_fusion, f32[1024]{0:T(1024)S(1)} %broadcast_multiply_fusion, bf16[512,1152]{1,0:T(8,128)(2,1)S(1)} %copy-done.14, bf16[512,1152]{1,0:T(8,128)(2,1)S(1)} %copy-done.8, bf16[1024,1728]{1,0:T(8,128)(2,1)S(1)} %copy-done.10, ...), kind=kOutput, calls=%fused_computation.19 | convolution fusion | flops 4087478272 | bytes 14763008 | tf_op jit(solution)/shard_map/dot_general | solution.py:22
  386.7 12.4 %all-to-all-done.4 = f32[16,1,6336]{2,1,0:T(1,128)S(1)} async-done(((f32[16,1,6336]{2,1,0:T(1,128)}), f32[16,1,6336]{2,1,0:T(1,128)S(1)}, u32[]{:S(2)}, u32[]{:S(2)}) %all-to-all-start.4) | async-done | bytes 405536 | tf_op jit(solution)/shard_map/all_to_all | solution.py:196
  399.4 7.4 %collective-permute-done.8 = bf16[512,1152]{1,0:T(8,128)(2,1)S(1)} collective-permute-done((bf16[512,1152]{1,0:T(8,128)(2,1)}, bf16[512,1152]{1,0:T(8,128)(2,1)S(1)}, u32[]{:S(2)}, u32[]{:S(2)}) %collective-permute-start.8) | collective-permute-done | bytes 1179680 | tf_op jit(solution)/shard_map/ppermute | solution.py:154
  424.9 7.5 %all-to-all-done.2 = bf16[16,2,1728]{2,1,0:T(2,128)(2,1)S(1)} async-done(((bf16[16,2,1728]{2,1,0:T(2,128)(2,1)}), bf16[16,2,1728]{2,1,0:T(2,128)(2,1)S(1)}, u32[]{:S(2)}, u32[]{:S(2)}) %all-to-all-start.2) | async-done | bytes 110624 | tf_op jit(solution)/shard_map/all_to_all | solution.py:196
  442.5 5.6 %all-to-all-done.3 = f32[16,1,72]{2,1,0:T(1,128)S(1)} async-done(((f32[16,1,72]{2,1,0:T(1,128)}), f32[16,1,72]{2,1,0:T(1,128)S(1)}, u32[]{:S(2)}, u32[]{:S(2)}) %all-to-all-start.3) | async-done | bytes 4640 | tf_op jit(solution)/shard_map/all_to_all | solution.py:196
  453.7 7.4 %reduce-scatter.10.cloned.1.call-done = bf16[72,2304]{1,0:T(8,128)(2,1)} async-done(((bf16[1152,2304]{1,0:T(8,128)(2,1)}), bf16[72,2304]{1,0:T(8,128)(2,1)}) %reduce-scatter.10.cloned.1.call-update) | async-done | bytes 331792
  (229 shorter events, 119.6 us)
Async XLA Ops:
  7.2 64.5 %all-gather.4.cloned.1.call-start = ((), (), s32[]{:S(2)}) async-start(), calls=%async_computation.8 | async-start | bytes 5640192 | tf_op jit(solution)/shard_map/all_gather | solution.py:232
  10.5 118.4 %all-gather.6.cloned.1.call-start = ((), (), s32[]{:S(2)}) async-start(), calls=%async_computation.9 | async-start | bytes 5640192 | tf_op jit(solution)/shard_map/all_gather | solution.py:233
  11.2 174.9 %all-gather.8.cloned.1.call-start = ((), (), s32[]{:S(2)}) async-start(), calls=%async_computation.10 | async-start | bytes 5640192 | tf_op jit(solution)/shard_map/all_gather | solution.py:234
  12.0 54.8 %collective-permute-start.1 = (bf16[512,1152]{1,0:T(8,128)(2,1)S(1)}, bf16[512,1152]{1,0:T(8,128)(2,1)S(1)}, u32[]{:S(2)}, u32[]{:S(2)}) collective-permute-start(bf16[512,1152]{1,0:T(8,128)(2,1)S(1)} %copy-done.7), channel_id=1, source_target_pairs={{0,1},{1,0},{2,3},{3,2},{4,5},{5,4},{6,7},{7,6},{8,9},{9,8},{10,11... | collective-permute-start | bytes 3538952 | tf_op jit(solution)/shard_map/ppermute | solution.py:154
  16.3 12.2 %all-to-all-start = ((bf16[16,1,72]{2,1,0:T(2,128)(2,1)}), bf16[16,1,72]{2,1,0:T(2,128)(2,1)S(1)}, u32[]{:S(2)}, u32[]{:S(2)}) async-start(bf16[16,1,72]{2,1,0:T(2,128)(2,1)} %transpose_reshape.4), calls=%async_computation | async-start | bytes 16384 | tf_op jit(solution)/shard_map/all_to_all | solution.py:196
  24.9 43.1 %copy-start.15 = (bf16[72,3456]{1,0:T(8,128)(2,1)}, bf16[72,3456]{1,0:T(8,128)(2,1)S(1)}, u32[]{:S(2)}) copy-start(bf16[72,3456]{1,0:T(8,128)(2,1)S(1)} %reshape.162) | copy-start | bytes 1492996
  29.7 12.9 %all-to-all-start.1 = ((f32[16,1,3456]{2,1,0:T(1,128)}), f32[16,1,3456]{2,1,0:T(1,128)S(1)}, u32[]{:S(2)}, u32[]{:S(2)}) async-start(f32[16,1,3456]{2,1,0:T(1,128)} %copy.85), calls=%async_computation.1 | async-start | bytes 442368 | tf_op jit(solution)/shard_map/all_to_all | solution.py:196
  33.2 416.7 %reduce-scatter.6.cloned.1.call-start = ((), (), s32[]{:S(2)}) async-start(), calls=%async_computation.11 | async-start | bytes 5640192 | tf_op jit(solution)/shard_map/reduce_scatter | solution.py:319
  33.3 58.5 %collective-permute-start.5 = (bf16[512,1152]{1,0:T(8,128)(2,1)}, bf16[512,1152]{1,0:T(8,128)(2,1)}, u32[]{:S(2)}, u32[]{:S(2)}) collective-permute-start(bf16[512,1152]{1,0:T(8,128)(2,1)} %param.25), channel_id=1, source_target_pairs={{0,1},{1,0},{2,3},{3,2},{4,5},{5,4},{6,7},{7,6},{8,9},{9,8},{10,11... | collective-permute-start | bytes 3538952 | tf_op jit(solution)/shard_map/ppermute | solution.py:154
  42.8 23.9 %collective-permute-start = (f32[1,6,576]{2,1,0:T(8,128)S(1)}, f32[1,6,576]{2,1,0:T(8,128)S(1)}, u32[]{:S(2)}, u32[]{:S(2)}) collective-permute-start(f32[1,6,576]{2,1,0:T(8,128)S(1)} %add_bitcast_fusion), channel_id=1, source_target_pairs={{0,1},{1,0},{2,3},{3,2},{4,5},{5,4},{6,7},{7,6},{8,9},{9,8},{10,11... | collective-permute-start | bytes 41480 | tf_op jit(solution)/shard_map/ppermute | solution.py:154
  90.0 28.2 %collective-permute-start.2 = (bf16[512,1152]{1,0:T(8,128)(2,1)S(1)}, bf16[512,1152]{1,0:T(8,128)(2,1)S(1)}, u32[]{:S(2)}, u32[]{:S(2)}) collective-permute-start(bf16[512,1152]{1,0:T(8,128)(2,1)S(1)} %convolution_convert_fusion.6), channel_id=1, source_target_pairs={{0,1},{1,0},{2,3},{3,2},{4,5},{5,4},{6,7},{7,6},{8,9},{9,8},{10,11... | collective-permute-start | bytes 3538952 | tf_op jit(solution)/shard_map/ppermute | solution.py:154
  103.4 188.0 %copy-start.1 = (bf16[512,576]{1,0:T(8,128)(2,1)}, bf16[512,576]{1,0:T(8,128)(2,1)S(1)}, u32[]{:S(2)}) copy-start(bf16[512,576]{1,0:T(8,128)(2,1)S(1)} %get-tuple-element.23.refs_2_) | copy-start | bytes 1769476
  123.1 63.1 %copy-start.25 = (bf16[512,1152]{1,0:T(8,128)(2,1)S(1)}, bf16[512,1152]{1,0:T(8,128)(2,1)}, u32[]{:S(2)}) copy-start(bf16[512,1152]{1,0:T(8,128)(2,1)} %get-tuple-element.144) | copy-start | bytes 3538948
  123.1 71.2 %collective-permute-start.3 = (bf16[512,1152]{1,0:T(8,128)(2,1)}, bf16[512,1152]{1,0:T(8,128)(2,1)}, u32[]{:S(2)}, u32[]{:S(2)}) collective-permute-start(bf16[512,1152]{1,0:T(8,128)(2,1)} %add_convert_fusion.2), channel_id=1, source_target_pairs={{0,1},{1,0},{2,3},{3,2},{4,5},{5,4},{6,7},{7,6},{8,9},{9,8},{10,11... | collective-permute-start | bytes 3538952 | tf_op jit(solution)/shard_map/ppermute | solution.py:154
  217.4 234.4 %reduce-scatter.8.cloned.1.call-start = ((), (), s32[]{:S(2)}) async-start(), calls=%async_computation.12 | async-start | bytes 5640192 | tf_op jit(solution)/shard_map/reduce_scatter | solution.py:319
  225.1 29.1 %collective-permute-start.6 = (bf16[512,1152]{1,0:T(8,128)(2,1)}, bf16[512,1152]{1,0:T(8,128)(2,1)}, u32[]{:S(2)}, u32[]{:S(2)}) collective-permute-start(bf16[512,1152]{1,0:T(8,128)(2,1)} %convolution_convert_fusion.4), channel_id=1, source_target_pairs={{0,1},{1,0},{2,3},{3,2},{4,5},{5,4},{6,7},{7,6},{8,9},{9,8},{10,11... | collective-permute-start | bytes 3538952 | tf_op jit(solution)/shard_map/ppermute | solution.py:154
  234.4 226.7 %reduce-scatter.10.cloned.1.call-start = ((), (), s32[]{:S(2)}) async-start(), calls=%async_computation.13 | async-start | bytes 5640192
  241.3 37.5 %collective-permute-start.4 = (bf16[512,1152]{1,0:T(8,128)(2,1)S(1)}, bf16[512,1152]{1,0:T(8,128)(2,1)S(1)}, u32[]{:S(2)}, u32[]{:S(2)}) collective-permute-start(bf16[512,1152]{1,0:T(8,128)(2,1)S(1)} %convolution_convert_fusion.5), channel_id=1, source_target_pairs={{0,1},{1,0},{2,3},{3,2},{4,5},{5,4},{6,7},{7,6},{8,9},{9,8},{10,11... | collective-permute-start | bytes 3538952 | tf_op jit(solution)/shard_map/ppermute | solution.py:154
  242.1 36.7 %slice-start = ((s8[5308416]{0:T(1024)(128)(4,1)}), s8[4194304]{0:T(1024)(128)(4,1)S(1)}, s32[]{:S(2)}) async-start(s8[5308416]{0:T(1024)(128)(4,1)} %bitcast.59), calls=%async_computation.14 | async-start | bytes 8388608
  242.1 36.7 %copy-start.24 = (bf16[512,1152]{1,0:T(8,128)(2,1)S(1)}, bf16[512,1152]{1,0:T(8,128)(2,1)}, u32[]{:S(2)}) copy-start(bf16[512,1152]{1,0:T(8,128)(2,1)} %param.25) | copy-start | bytes 3538948
  242.1 36.7 %slice-start.1 = ((s8[5308416]{0:T(1024)(128)(4,1)}), s8[1114112]{0:T(1024)(128)(4,1)S(1)}, s32[]{:S(2)}) async-start(s8[5308416]{0:T(1024)(128)(4,1)} %bitcast.59), calls=%async_computation.15 | async-start | bytes 2228224
  242.1 36.7 %copy-start.43 = (bf16[512,2304]{1,0:T(8,128)(2,1)S(1)}, bf16[512,2304]{1,0:T(8,128)(2,1)}, u32[]{:S(2)}) copy-start(bf16[512,2304]{1,0:T(8,128)(2,1)} %get-tuple-element.165) | copy-start | bytes 7077892
  286.3 27.7 %collective-permute-start.7 = (bf16[512,1152]{1,0:T(8,128)(2,1)}, bf16[512,1152]{1,0:T(8,128)(2,1)}, u32[]{:S(2)}, u32[]{:S(2)}) collective-permute-start(bf16[512,1152]{1,0:T(8,128)(2,1)} %get-tuple-element.152), channel_id=1, source_target_pairs={{0,1},{1,0},{2,3},{3,2},{4,5},{5,4},{6,7},{7,6},{8,9},{9,8},{10,11... | collective-permute-start | bytes 3538952 | tf_op jit(solution)/shard_map/ppermute | solution.py:154
  363.4 4.6 collective-permute-start.11
  380.3 26.5 %collective-permute-start.8 = (bf16[512,1152]{1,0:T(8,128)(2,1)}, bf16[512,1152]{1,0:T(8,128)(2,1)S(1)}, u32[]{:S(2)}, u32[]{:S(2)}) collective-permute-start(bf16[512,1152]{1,0:T(8,128)(2,1)} %slice.141), channel_id=1, source_target_pairs={{0,1},{1,0},{2,3},{3,2},{4,5},{5,4},{6,7},{7,6},{8,9},{9,8},{10,11... | collective-permute-start | bytes 3538952 | tf_op jit(solution)/shard_map/ppermute | solution.py:154
  382.8 16.3 %all-to-all-start.4 = ((f32[16,1,6336]{2,1,0:T(1,128)}), f32[16,1,6336]{2,1,0:T(1,128)S(1)}, u32[]{:S(2)}, u32[]{:S(2)}) async-start(f32[16,1,6336]{2,1,0:T(1,128)} %broadcast_in_dim.11), calls=%async_computation.4 | async-start | bytes 819200 | tf_op jit(solution)/shard_map/all_to_all | solution.py:196
  413.9 35.4 %copy-start.32 = (bf16[1,1152]{1,0:T(2,128)(2,1)S(1)}, bf16[1,1152]{1,0:T(2,128)(2,1)}, u32[]{:S(2)}) copy-start(bf16[1,1152]{1,0:T(2,128)(2,1)} %param.14) | copy-start | bytes 6916
  413.9 35.4 %copy-start.33 = (f32[1,1152]{1,0:T(1,128)S(1)}, f32[1,1152]{1,0:T(1,128)}, u32[]{:S(2)}) copy-start(f32[1,1152]{1,0:T(1,128)} %get-tuple-element.148) | copy-start | bytes 13828
  414.1 3.8 collective-permute-start.9
  420.7 11.6 %all-to-all-start.2 = ((bf16[16,2,1728]{2,1,0:T(2,128)(2,1)}), bf16[16,2,1728]{2,1,0:T(2,128)(2,1)S(1)}, u32[]{:S(2)}, u32[]{:S(2)}) async-start(bf16[16,2,1728]{2,1,0:T(2,128)(2,1)} %reshape.192), calls=%async_computation.2 | async-start | bytes 229376 | tf_op jit(solution)/shard_map/all_to_all | solution.py:196
  432.9 3.7 collective-permute-start.10
  437.2 10.9 %all-to-all-start.3 = ((f32[16,1,72]{2,1,0:T(1,128)}), f32[16,1,72]{2,1,0:T(1,128)S(1)}, u32[]{:S(2)}, u32[]{:S(2)}) async-start(f32[16,1,72]{2,1,0:T(1,128)} %bitcast.5), calls=%async_computation.3 | async-start | bytes 16384 | tf_op jit(solution)/shard_map/all_to_all | solution.py:196
  (38 other events, 344.0 us)
Sparse Core Ops, SparseCore 0:
  10.8 60.8 all-gather.3
  73.9 54.9 all-gather.5
  131.0 55.0 all-gather.7
  217.6 78.2 reduce-scatter.5
  299.7 78.5 reduce-scatter.7
  382.2 78.8 reduce-scatter.9

commit v2 on v1

--- a/solution.py
+++ b/solution.py
@@ -14,6 +14,7 @@
 EPS = 1e-06
 LOG2E = math.log2(math.e)
 VMEM_LIMIT = 48 * 1024 * 1024
+TILE = 768
 BOTH_LAST = (((1,), (1,)), ((), ()))
 BOTH_FIRST = (((0,), (0,)), ((), ()))
 
@@ -93,11 +94,12 @@
 
 
 def attend_back_kernel(start, last, *refs):
+    packed_ref, up_ref, heads_ref, log_ref = refs[:4]
+    rows, cols = up_ref.shape
     if last:
-        packed_ref, up_ref, heads_ref, log_ref, key_in, value_in, query_ref, key_ref, value_ref = refs
+        query_ins, key_in, value_in, out_ref, sum_ref = refs[4:-4], *refs[-4:]
     else:
-        packed_ref, up_ref, heads_ref, log_ref, query_ref, key_ref, value_ref = refs
-    rows, cols = up_ref.shape
+        query_ref, key_ref, value_ref = refs[4:]
     scale = 1.0 / math.sqrt(HD)
     factor = LOG2E * scale
     products = (up_ref[...].astype(jnp.float32) * heads_ref[...].astype(jnp.float32)).T
@@ -119,28 +121,45 @@
         if last:
             value_grad += value_in[:, here]
             key_grad += key_in[:, here]
-        value_ref[:, here] = value_grad.astype(value_ref.dtype)
-        key_ref[:, here] = key_grad.astype(key_ref.dtype)
+            out_ref[:, 2 * cols + at : 2 * cols + at + HD] = value_grad.astype(jnp.bfloat16)
+            out_ref[:, cols + at : cols + at + HD] = key_grad.astype(jnp.bfloat16)
+        else:
+            value_ref[:, here] = value_grad
+            key_ref[:, here] = key_grad
         pieces.append(mm(key_rows, score_grads, BOTH_FIRST) * scale)
-    query_ref[...] = jnp.concatenate(pieces, axis=0).T.astype(jnp.bfloat16)
-
-
-def attend_back(packed, start, upstream, heads_low, logs, sums, last):
+    query_grad = jnp.concatenate(pieces, axis=0).T.astype(jnp.bfloat16)
+    if last:
+        for step, query_in in enumerate(query_ins):
+            out_ref[step * rows : (step + 1) * rows, :cols] = query_in[...]
+        out_ref[start : start + rows, :cols] = query_grad
+        sum_ref[...] = jnp.sum(out_ref[...].astype(jnp.float32), axis=0, keepdims=True)
+    else:
+        query_ref[...] = query_grad
+
+
+def attend_back(packed, start, upstream, heads_low, logs, query_grads, sums, last):
     length, width = packed.shape
     cols = width // 3
     heads = cols // HD
     rows = upstream.shape[0]
-    kind = jnp.bfloat16 if last else jnp.float32
-    operands = (packed, upstream, heads_low, logs) + (sums if last else ())
+    operands = (packed, upstream, heads_low, logs)
+    if last:
+        operands += tuple(query_grads) + tuple(sums)
+        shapes = (
+            jax.ShapeDtypeStruct((length, width), jnp.bfloat16),
+            jax.ShapeDtypeStruct((1, width), jnp.float32),
+        )
+    else:
+        shapes = (
+            jax.ShapeDtypeStruct((rows, cols), jnp.bfloat16),
+            jax.ShapeDtypeStruct((length, cols), jnp.float32),
+            jax.ShapeDtypeStruct((length, cols), jnp.float32),
+        )
     return pl.pallas_call(
         functools.partial(attend_back_kernel, start, last),
-        out_shape=(
-            jax.ShapeDtypeStruct((rows, cols), jnp.bfloat16),
-            jax.ShapeDtypeStruct((length, cols), kind),
-            jax.ShapeDtypeStruct((length, cols), kind),
-        ),
+        out_shape=shapes,
         in_specs=[pl.BlockSpec(memory_space=pltpu.VMEM)] * len(operands),
-        out_specs=(pl.BlockSpec(memory_space=pltpu.VMEM),) * 3,
+        out_specs=jax.tree.map(lambda _: pl.BlockSpec(memory_space=pltpu.VMEM), shapes),
         compiler_params=pltpu.CompilerParams(vmem_limit_bytes=VMEM_LIMIT),
         cost_estimate=pl.CostEstimate(
             flops=10 * rows * length * 256 * heads,
@@ -148,6 +167,133 @@
             transcendentals=rows * length * heads,
         ),
     )(*operands)
+
+
+def feed_kernel(second_ref, feed_ref, up_ref, down_ref, bias_ref, act_ref, pre_ref, sum_ref):
+    act, slope = gelu_pair(mm(second_ref[...], up_ref[...]) + bias_ref[...])
+    act_ref[...] = act.astype(jnp.bfloat16)
+    low = (mm(feed_ref[...], down_ref[...]) * slope).astype(jnp.bfloat16)
+    pre_ref[...] = low
+    sum_ref[...] = jnp.sum(low.astype(jnp.float32), axis=0, keepdims=True)
+
+
+def feed_forward(second, feed_grad, weights, bias):
+    rows, width = second.shape
+    hidden = weights.shape[1] // 2
+    tile = TILE
+    tiles = hidden // tile
+    if hidden % tile:
+        act, slope = gelu_pair(mm(second, weights[:, :hidden]) + bias)
+        low = (mm(feed_grad, weights[:, hidden:]) * slope).astype(jnp.bfloat16)
+        sums = jnp.sum(low, axis=0, keepdims=True, dtype=jnp.float32)
+        return act.astype(jnp.bfloat16), low, sums
+    whole = pl.BlockSpec((rows, width), lambda j: (0, 0))
+    piece = pl.BlockSpec((rows, tile), lambda j: (0, j))
+    line = pl.BlockSpec((1, tile), lambda j: (0, j))
+    return pl.pallas_call(
+        feed_kernel,
+        grid=(tiles,),
+        out_shape=(
+            jax.ShapeDtypeStruct((rows, hidden), jnp.bfloat16),
+            jax.ShapeDtypeStruct((rows, hidden), jnp.bfloat16),
+            jax.ShapeDtypeStruct((1, hidden), jnp.float32),
+        ),
+        in_specs=[
+            whole,
+            whole,
+            pl.BlockSpec((width, tile), lambda j: (0, j)),
+            pl.BlockSpec((width, tile), lambda j: (0, j + tiles)),
+            line,
+        ],
+        out_specs=(piece, piece, line),
+        compiler_params=pltpu.CompilerParams(vmem_limit_bytes=VMEM_LIMIT),
+        cost_estimate=pl.CostEstimate(
+            flops=4 * rows * width * hidden,
+            bytes_accessed=2 * (2 * second.size + weights.size + 2 * rows * hidden),
+            transcendentals=rows * hidden,
+        ),
+    )(second, feed_grad, weights, weights, bias)
+
+
+def feed_weight_kernel(tiles, feed_ref, second_ref, act_ref, pre_ref, out_ref, turned_ref):
+    step = pl.program_id(0)
+
+    @pl.when(step == 0)
+    def _():
+        turned_ref[...] = feed_ref[...].T
+
+    @pl.when(step == tiles)
+    def _():
+        turned_ref[...] = second_ref[...].T
+
+    @pl.when(step < tiles)
+    def _():
+        out_ref[...] = mm(turned_ref[...], act_ref[...]).astype(jnp.bfloat16)
+
+    @pl.when(step >= tiles)
+    def _():
+        out_ref[...] = mm(turned_ref[...], pre_ref[...]).astype(jnp.bfloat16)
+
+
+def feed_weight_grads(feed_grad, second, act, pre):
+    rows, width = second.shape
+    hidden = act.shape[1]
+    tile = TILE
+    tiles = hidden // tile
+    if hidden % tile:
+        grads = [mm(feed_grad, act, BOTH_FIRST), mm(second, pre, BOTH_FIRST)]
+        return jnp.concatenate(grads, axis=1).astype(jnp.bfloat16)
+    whole = pl.BlockSpec((rows, width), lambda j: (0, 0))
+    return pl.pallas_call(
+        functools.partial(feed_weight_kernel, tiles),
+        grid=(2 * tiles,),
+        out_shape=jax.ShapeDtypeStruct((width, 2 * hidden), jnp.bfloat16),
+        in_specs=[
+            whole,
+            whole,
+            pl.BlockSpec((rows, tile), lambda j: (0, jnp.minimum(j, tiles - 1))),
+            pl.BlockSpec((rows, tile), lambda j: (0, jnp.maximum(j - tiles, 0))),
+        ],
+        out_specs=pl.BlockSpec((width, tile), lambda j: (0, j)),
+        scratch_shapes=[pltpu.VMEM((width, rows), jnp.bfloat16)],
+        compiler_params=pltpu.CompilerParams(vmem_limit_bytes=VMEM_LIMIT),
+        cost_estimate=pl.CostEstimate(
+            flops=4 * rows * width * hidden,
+            bytes_accessed=4 * (second.size + act.size + width * hidden),
+            transcendentals=0,
+        ),
+    )(feed_grad, second, act, pre)
+
+
+def weight_kernel(first_ref, packed_ref, upstream_ref, heads_ref, out_ref):
+    width, wide = out_ref.shape
+    cut = packed_ref.shape[1]
+    step = width // 3
+
+    def body(index, carry):
+        rows = pl.ds(pl.multiple_of(index * step, step), step)
+        out_ref[rows, :cut] = mm(first_ref[:, rows], packed_ref[...], BOTH_FIRST).astype(jnp.bfloat16)
+        out_ref[rows, cut:] = mm(upstream_ref[:, rows], heads_ref[...], BOTH_FIRST).astype(jnp.bfloat16)
+        return carry
+
+    lax.fori_loop(0, width // step, body, 0)
+
+
+def weight_grads(first, packed, upstream, heads):
+    width = first.shape[1]
+    wide = packed.shape[1] + heads.shape[1]
+    return pl.pallas_call(
+        weight_kernel,
+        out_shape=jax.ShapeDtypeStruct((width, wide), jnp.bfloat16),
+        in_specs=[pl.BlockSpec(memory_space=pltpu.VMEM)] * 4,
+        out_specs=pl.BlockSpec(memory_space=pltpu.VMEM),
+        compiler_params=pltpu.CompilerParams(vmem_limit_bytes=VMEM_LIMIT),
+        cost_estimate=pl.CostEstimate(
+            flops=2 * first.shape[0] * width * wide,
+            bytes_accessed=2 * (first.size + packed.size + upstream.size + heads.size + width * wide),
+            transcendentals=0,
+        ),
+    )(first, packed, upstream, heads)
 
 
 def swap(values):
@@ -175,15 +321,12 @@
     return lax.all_gather(own, "tp", axis=own.ndim - 1, tiled=True)
 
 
-def scatter_columns(whole):
+def take_columns(whole):
     count = lax.axis_size("tp")
+    piece = whole.shape[1] // count
     if count == 2:
-        width = whole.shape[-1] // 2
-        left = lax.axis_index("tp") == 0
-        halves = whole[..., :width], whole[..., width:]
-        own = jnp.where(left, halves[0], halves[1])
-        return own + swap(jnp.where(left, halves[1], halves[0]))
-    return lax.psum_scatter(whole, "tp", scatter_dimension=whole.ndim - 1, tiled=True)
+        return jnp.where(lax.axis_index("tp") == 0, whole[:, :piece], whole[:, piece:])
+    return lax.dynamic_slice_in_dim(whole, lax.axis_index("tp") * piece, piece, 1)
 
 
 def sum_pair(values):
@@ -198,6 +341,21 @@
 
 def share(values):
     return exchange(jnp.broadcast_to(values[None], (lax.axis_size("fsdp"),) + values.shape))
+
+
+def hop(values, z_step, x_step, core_step):
+    planes = lax.axis_size("fsdp") // 4
+    moves = []
+    for source in range(4 * planes):
+        z, x, core = source // 4, source // 2 % 2, source % 2
+        target = ((z + z_step) % planes * 2 + (x + x_step) % 2) * 2 + (core + core_step) % 2
+        moves.append((source, target))
+    return lax.ppermute(values, "fsdp", moves)
+
+
+def place():
+    index = lax.axis_index("fsdp")
+    return index // 4, index // 2 % 2, index % 2
 
 
 def per_device(
@@ -230,10 +388,11 @@
 
     first_shard = jnp.concatenate([attention_weight.reshape(depth, 3 * cols), output_weight.T], axis=1)
     first_weights = lax.all_gather(first_shard, "fsdp", axis=0, tiled=True)
-    up_all = lax.all_gather(up_weight, "fsdp", axis=0, tiled=True)
-    down_all = lax.all_gather(down_weight.T, "fsdp", axis=0, tiled=True)
     attention_all = first_weights[:, : 3 * cols]
     output_all = first_weights[:, 3 * cols :]
+    feed_shard = jnp.concatenate([up_weight, down_weight.T], axis=1)
+
+    inputs_parts = gather_rows(inputs, paired)
 
     condition_values = conditions.astype(f32)
     silu_low = jax.nn.silu(condition_values).astype(bf16)
@@ -242,7 +401,12 @@
     modulation_flat = modulation_weight.reshape(depth, 6 * cols)
     partial = mm(silu_rows, modulation_flat).reshape(fsdp, latents, 6 * cols)
     own_columns = jnp.sum(exchange(partial), axis=0).reshape(latents, 6, cols)
+    own_columns, inputs_parts = lax.optimization_barrier((own_columns, inputs_parts))
     modulation = gather_columns(own_columns + modulation_bias.astype(f32))
+    feed_shard, modulation = lax.optimization_barrier((feed_shard, modulation))
+    feed_weights = lax.all_gather(feed_shard, "fsdp", axis=0, tiled=True)
+    up_all = feed_weights[:, :hidden]
+    down_all = feed_weights[:, hidden:]
     own_modulation = modulation[0]
     if latents > 1:
         own_modulation = lax.dynamic_index_in_dim(
@@ -267,8 +431,9 @@
         mine = jnp.arange(latents)[:, None] == rank * local_rows // length
         return jnp.where(mine, total, 0.0)
 
-    inputs_all = jnp.concatenate(gather_rows(inputs, paired), axis=0)
-    cotangent_parts = gather_rows(cotangent, paired)
+    cotangent_late, inputs_parts = lax.optimization_barrier((cotangent, inputs_parts))
+    inputs_all = jnp.concatenate(inputs_parts, axis=0)
+    cotangent_parts = gather_rows(cotangent_late, paired)
     input_values = inputs.astype(f32)
     first_normed, first_inverse = normalize(input_values)
     first_normed_all, _ = normalize(inputs_all.astype(f32))
@@ -276,6 +441,7 @@
     bias_rows = attention_bias.astype(f32)
     packed_bias = jnp.concatenate([bias_rows[0], jnp.zeros((cols,), f32), bias_rows[1]])
     packed = (mm(first_all, attention_all) + packed_bias).astype(bf16)
+    packed, cotangent_parts = lax.optimization_barrier((packed, cotangent_parts))
 
     block = local_rows
     blocks = length // block
@@ -298,81 +464,84 @@
         feed_parts = [(gate_all * part.astype(f32)).astype(bf16) for part in cotangent_parts]
     else:
         feed_parts = [(gate_all * cotangent_parts[0].astype(f32)).astype(bf16)]
-    up_bias_row = up_bias.astype(f32)[None]
-    act_parts = []
-    pre_parts = []
-    for second, feed_grad in zip(second_parts, feed_parts):
-        act, slope = gelu_pair(mm(second, up_all) + up_bias_row)
-        act_parts.append(act.astype(bf16))
-        pre_parts.append((mm(feed_grad, down_all) * slope).astype(bf16))
-    second_grad = scatter_rows([mm(part, up_all, BOTH_LAST) for part in pre_parts], paired)
-    feed = scatter_rows([mm(part, down_all, BOTH_LAST) for part in act_parts], paired)
-    feed = feed + down_bias.astype(f32)
-    outputs = (mid + own_rows(5) * feed).astype(bf16)
-
     feed_all = jnp.concatenate(feed_parts, axis=0)
-    act_all = jnp.concatenate(act_parts, axis=0)
-    pre_all = jnp.concatenate(pre_parts, axis=0)
     second_all = jnp.concatenate(second_parts, axis=0)
+    act_all, pre_all, pre_sum = feed_forward(
+        second_all, feed_all, feed_weights, up_bias.astype(f32)[None]
+    )
+    feed_grads = feed_weight_grads(feed_all, second_all, act_all, pre_all)
 
     def scatter_weights(values):
         return lax.psum_scatter(
             values.astype(bf16), "fsdp", scatter_dimension=0, tiled=True
         ).astype(f32)
 
-    grad_down = scatter_weights(mm(feed_all, act_all, BOTH_FIRST))
-    grad_up_weight = scatter_weights(mm(second_all, pre_all, BOTH_FIRST))
-
+    feed_grads, act_all, pre_all = lax.optimization_barrier((feed_grads, act_all, pre_all))
+    feed_grads = scatter_weights(feed_grads)
+    rows_kept = local_rows if paired else local_rows * tp
+    act_parts = [act_all[:rows_kept], act_all[rows_kept:]][: len(second_parts)]
+    pre_parts = [pre_all[:rows_kept], pre_all[rows_kept:]][: len(second_parts)]
+    feed_sums = [mm(part, down_all, BOTH_LAST) for part in act_parts]
+    second_sums = [mm(part, up_all, BOTH_LAST) for part in pre_parts]
+
+    second_grad = scatter_rows(second_sums, paired)
     upstream = cotangent.astype(f32)
     mid_grad = upstream + normalize_back(
         second_grad * (1.0 + own_rows(4)), second_normed, second_inverse
     )
     attention_low = (own_rows(2) * mid_grad).astype(bf16)
     upstream_parts = gather_rows(attention_low, paired)
+    if paired:
+        feed_sums[1] = feed_sums[1].astype(bf16)
+        feed_sums[1], upstream_parts[1] = lax.optimization_barrier((feed_sums[1], upstream_parts[1]))
+    feed = scatter_rows(feed_sums, paired) + down_bias.astype(f32)
     if paired:
         heads_grads = [mm(part, output_all).astype(bf16) for part in upstream_parts]
     else:
         heads_grad = mm(upstream_parts[0], output_all).astype(bf16)
         heads_grads = [heads_grad[n * block : (n + 1) * block] for n in range(group_blocks)]
-    query_grads = []
-    key_grads = []
-    value_grads = []
+    packed_parts = []
+    packed_sums = []
     for latent in range(latents):
-        sums = ()
+        query_grads = []
+        sums = (jnp.zeros((length, cols), f32),) * 2
         for step in range(blocks):
             at = latent * blocks + step
-            query_grad, *sums = attend_back(
+            result = attend_back(
                 packed_latents[latent],
                 step * block,
                 heads_grads[at],
                 heads_parts[at],
                 logs[at],
-                tuple(sums),
+                query_grads,
+                sums,
                 step == blocks - 1,
             )
-            query_grads.append(query_grad)
-        key_grads.append(sums[0])
-        value_grads.append(sums[1])
-    packed_low = jnp.concatenate(
-        [jnp.concatenate(part, axis=0) for part in (query_grads, key_grads, value_grads)], axis=1
-    )
+            if step < blocks - 1:
+                query_grads.append(result[0])
+                sums = result[1:] if step == 0 else tuple(map(jnp.add, sums, result[1:]))
+        packed_parts.append(result[0])
+        packed_sums.append(result[1])
+    packed_low = packed_parts[0] if latents == 1 else jnp.concatenate(packed_parts, axis=0)
+    packed_sum = jnp.sum(jnp.concatenate(packed_sums, axis=0), axis=0)
+    first_grads = weight_grads(
+        first_all,
+        packed_low,
+        jnp.concatenate(upstream_parts, axis=0),
+        jnp.concatenate(heads_parts, axis=0),
+    )
+    first_grads, feed, packed_low = lax.optimization_barrier((first_grads, feed, packed_low))
+    first_grads, feed_grads = lax.optimization_barrier((first_grads, feed_grads))
+    first_grads = scatter_weights(first_grads)
+    grad_attention = first_grads[:, : 3 * cols]
+    grad_output = first_grads[:, 3 * cols :].T
+    outputs = (mid + own_rows(5) * feed).astype(bf16)
     first_grad_all = mm(packed_low, attention_all, BOTH_LAST)
-    attention_grad = mm(first_all, packed_low, BOTH_FIRST)
-    output_grad = mm(
-        jnp.concatenate(upstream_parts, axis=0), jnp.concatenate(heads_parts, axis=0), BOTH_FIRST
-    )
-    first_grads = scatter_weights(jnp.concatenate([attention_grad, output_grad], axis=1))
-
-    if paired:
-        first_grad_parts = [first_grad_all[:local_rows], first_grad_all[local_rows:]]
-    else:
-        first_grad_parts = [first_grad_all]
-    first_grad = scatter_rows(first_grad_parts, paired)
-    grad_inputs = mid_grad + normalize_back(
-        first_grad * (1.0 + own_rows(1)), first_normed, first_inverse
-    )
-
-    modulation_parts = jnp.stack(
+
+    own_feed = feed_parts[0]
+    if not paired:
+        own_feed = (own_rows(5) * upstream).astype(bf16)
+    token_sums = jnp.stack(
         [
             sum_latents(first_grad_all),
             sum_latents(first_grad_all * first_normed_all),
@@ -383,36 +552,43 @@
         ],
         axis=1,
     )
-    modulation_low = scatter_columns(modulation_parts).astype(bf16)
-    modulation_all = share(modulation_low.reshape(latents, 6 * cols)).reshape(
-        fsdp * latents, 6 * cols
-    )
+    token_sums = jnp.concatenate(
+        [
+            token_sums.reshape(latents * 6, width),
+            jnp.sum(attention_low, axis=0, dtype=f32, keepdims=True),
+            jnp.sum(own_feed, axis=0, dtype=f32, keepdims=True),
+        ]
+    )
+    token_sums = sum_pair(token_sums)
+    first_grad_all, token_sums = lax.optimization_barrier((first_grad_all, token_sums))
+    if paired:
+        first_grad_parts = [first_grad_all[:local_rows], first_grad_all[local_rows:]]
+    else:
+        first_grad_parts = [first_grad_all]
+    first_grad = scatter_rows(first_grad_parts, paired)
+    modulation_low = take_columns(token_sums[: latents * 6]).astype(bf16)
+    sums = jnp.concatenate(
+        [
+            modulation_low.astype(f32).reshape(latents * 6 * cols),
+            token_sums[latents * 6 :].reshape(2 * width),
+            packed_sum,
+            pre_sum[0],
+        ]
+    )
+    shared = share(sums[None]).reshape(fsdp, -1)
+    shared, first_grad = lax.optimization_barrier((shared, first_grad))
+    modulation_all = shared[:, : latents * 6 * cols].reshape(fsdp * latents, 6 * cols).astype(bf16)
+    bias_sums = jnp.sum(shared[:, latents * 6 * cols :], axis=0)
     grad_modulation_weight = mm(silu_rows, modulation_all, BOTH_FIRST).reshape(depth, 6, cols)
     grad_modulation_bias = jnp.sum(modulation_all, axis=0, dtype=f32).reshape(6, cols)
     silu_part = sum_pair(mm(modulation_all, modulation_flat, BOTH_LAST))
     silu_total = exchange(silu_part.reshape(fsdp, latents, depth))
     silu_total = silu_total.transpose(1, 0, 2).reshape(latents, width)
+    grad_inputs = mid_grad + normalize_back(
+        first_grad * (1.0 + own_rows(1)), first_normed, first_inverse
+    )
     grad_conditions = silu_total * silu_slope(condition_values)
 
-    own_feed = feed_parts[0]
-    if not paired:
-        own_feed = (own_rows(5) * upstream).astype(bf16)
-    token_sums = sum_pair(
-        jnp.concatenate(
-            [
-                jnp.sum(attention_low, axis=0, dtype=f32),
-                jnp.sum(own_feed, axis=0, dtype=f32),
-            ]
-        )
-    )
-    bias_parts = jnp.concatenate(
-        [
-            token_sums,
-            jnp.sum(packed_low, axis=0, dtype=f32),
-            jnp.sum(pre_all, axis=0, dtype=f32),
-        ]
-    )
-    bias_sums = jnp.sum(share(bias_parts), axis=0)
     grad_output_bias = bias_sums[:width]
     grad_down_bias = bias_sums[width : 2 * width]
     packed_sums = bias_sums[2 * width : 2 * width + 3 * cols]
@@ -424,13 +600,13 @@
         grad_conditions,
         grad_modulation_weight,
         grad_modulation_bias,
-        first_grads[:, : 3 * cols].reshape(depth, 3, cols),
+        grad_attention.reshape(depth, 3, cols),
         grad_attention_bias,
-        first_grads[:, 3 * cols :].T,
+        grad_output,
         grad_output_bias,
-        grad_up_weight,
+        feed_grads[:, hidden:],
         grad_up_bias,
-        grad_down.T,
+        feed_grads[:, :hidden].T,
         grad_down_bias,
     )
 

time: 478 us -> 429 us (0.90)
  matrix products: 116 us -> 55.6 us
  waiting for transfers between devices: 188 us -> 129 us
  Pallas kernels: 45.4 us -> 91.8 us
  other arithmetic: 31.7 us -> 48.4 us
  blocking collectives: 0 us -> 13.3 us
  local copies, waits for them, and re-layouts: 39.4 us -> 33.8 us
    dot_general x21 -> x13, matrix products: 116 us -> 55.6 us  [mm(): return lax.dot_general(a, b, dims, preferred_element_type=jnp.float32)]
    pallas_call x0 -> x3, Pallas kernels: none -> 44.8 us  [the longest x1 17 us: feed_weight_grads(): pl.pallas_call(functools.partial(feed_weight_kernel, tiles), grid=(2 * ti...]
    all_gather x2 -> x1, waiting for transfers between devices: 51.8 us -> 10.6 us  [per_device(): feed_weights = lax.all_gather(feed_shard, 'fsdp', axis=0, tiled=True)]
    ppermute x12 -> x11, waiting for transfers between devices: 86.1 us -> 65.3 us  [swap(): return lax.ppermute(values, 'tp', [(0, 1), (1, 0)])]
    all_gather x1, waiting for transfers between devices: 3.72 us -> 21.2 us  [per_device(): first_weights = lax.all_gather(first_shard, 'fsdp', axis=0, tiled=True)]
    all_to_all x0 -> x1, blocking collectives: none -> 13.3 us  [exchange(): return lax.all_to_all(blocks, 'fsdp', 0, 0, tiled=True)]
    all_to_all x5 -> x3, waiting for transfers between devices: 37.8 us -> 26.2 us  [exchange(): return lax.all_to_all(blocks, 'fsdp', 0, 0, tiled=True)]
    add x0 -> x4, other arithmetic: none -> 8.92 us  [the longest x1 3.81 us: per_device(): feed = scatter_rows(feed_sums, paired) + down_bias.astype(f32)]
  transfers between devices with their start and end apart: 23 -> 18, of which waited for: 17 -> 13; matrix products, arithmetic and copies ran while one was open for 33% -> 28% of each run, Pallas kernels for 10% -> 14%
where the time goes in v2:
time: 429 us; the launch traced here: 422 us
  waiting for transfers between devices  129 us (30%)
  Pallas kernels  91.8 us (21%)
  matrix products  55.6 us (13%)
  other arithmetic  48.4 us (11%)
  starting transfers between devices  35.5 us (8%)
  local copies, waits for them, and re-layouts  33.8 us (8%)
  between operations  14.7 us (3%)
  blocking collectives  13.3 us (3%)
    ppermute x11, waiting for transfers between devices, swap(): return lax.ppermute(values, 'tp', [(0, 1), (1, 0)])  65.3 us
    dot_general x13, matrix products, mm(): return lax.dot_general(a, b, dims, preferred_element_type=jnp.float32)  55.6 us
    pallas_call x2, Pallas kernels, attend_back(): pl.pallas_call(functools.partial(attend_back_kernel, start, last), out_sh...  30.7 us
    all_to_all x3, waiting for transfers between devices, exchange(): return lax.all_to_all(blocks, 'fsdp', 0, 0, tiled=True)  26.2 us
    all_gather x1, waiting for transfers between devices, per_device(): first_weights = lax.all_gather(first_shard, 'fsdp', axis=0, tiled=True)  21.2 us
    all_to_all x3, starting transfers between devices, exchange(): return lax.all_to_all(blocks, 'fsdp', 0, 0, tiled=True)  20.5 us
    pallas_call x1, Pallas kernels, feed_weight_grads(): pl.pallas_call(functools.partial(feed_weight_kernel, tiles), grid=(2 * ti...  17 us
    pallas_call x1, Pallas kernels, feed_forward(): pl.pallas_call(feed_kernel, grid=(tiles,), out_shape=(jax.ShapeDtypeStruc...  16.3 us
  transfers between devices with their start and end apart: 18, of which 13 were waited for; matrix products, arithmetic and copies ran while one was open for 28% of the time, Pallas kernels for 14%

profile of v2, /device:TPU:0, one launch (start us, length us, event | category | flops | bytes accessed | tf_op | source)
XLA Modules:
  0.0 422.4 jit_solution(5757541947446554478)
XLA Ops:
  15.4 5.9 %all-to-all-start = ((bf16[16,1,72]{2,1,0:T(2,128)(2,1)}), bf16[16,1,72]{2,1,0:T(2,128)(2,1)S(1)}, u32[]{:S(2)}, u32[]{:S(2)}) async-start(bf16[16,1,72]{2,1,0:T(2,128)(2,1)} %transpose_reshape.4), calls=%async_computation | async-start | bytes 16384 | tf_op jit(solution)/shard_map/all_to_all | solution.py:339
  22.0 5.7 %all-to-all-done = bf16[16,1,72]{2,1,0:T(2,128)(2,1)S(1)} async-done(((bf16[16,1,72]{2,1,0:T(2,128)(2,1)}), bf16[16,1,72]{2,1,0:T(2,128)(2,1)S(1)}, u32[]{:S(2)}, u32[]{:S(2)}) %all-to-all-start) | async-done | bytes 2336 | tf_op jit(solution)/shard_map/all_to_all | solution.py:339
  28.1 13.3 %all_to_all.20 = f32[16,1,3456]{2,1,0:T(1,128)S(1)} all-to-all(f32[16,1,3456]{2,1,0:T(1,128)S(1)} %copy.58), channel_id=1, replica_groups=mesh['fsdp'=16,'tp'=2] {'fsdp'}, dimensions={0} | all-to-all | bytes 442368 | tf_op jit(solution)/shard_map/all_to_all | solution.py:339
  52.5 21.2 %all-gather.3.cloned.1.call-done = bf16[1152,2304]{1,0:T(8,128)(2,1)} async-done(((bf16[72,2304]{1,0:T(8,128)(2,1)}), bf16[1152,2304]{1,0:T(8,128)(2,1)}) %all-gather.3.cloned.1.call-update) | async-done | bytes 5308432 | tf_op jit(solution)/shard_map/all_gather | solution.py:390
  73.7 7.5 %add_convert_fusion.packed_ref.refs_0_ = bf16[1024,1728]{1,0:T(8,128)(2,1)S(1)} fusion(bf16[1024,1152]{1,0:T(8,128)(2,1)S(1)} %fusion.5.first_ref, f32[1728]{0:T(1024)} %concatenate.37, bf16[1152,2304]{1,0:T(8,128)(2,1)} %all-gather.3.cloned.1.call-done), kind=kOutput, calls=%fused_computation | convolution fusion | flops 4080402432 | bytes 10035200 | tf_op jit(solution)/shard_map/dot_general | solution.py:23
  81.2 7.9 %shard_map.229 = (bf16[512,576]{1,0:T(8,128)(2,1)S(1)}, f32[8,512]{1,0:T(8,128)S(1)}) custom-call(bf16[1024,1728]{1,0:T(8,128)(2,1)S(1)} %add_convert_fusion.packed_ref.refs_0_), custom_call_target="tpu_custom_call" | custom-call | flops 4294967296 | bytes 4128768 | tf_op jit(solution)/shard_map/pallas_call | solution.py:79
  93.2 8.4 %shard_map.228 = (bf16[512,576]{1,0:T(8,128)(2,1)S(1)}, f32[8,512]{1,0:T(8,128)S(1)}) custom-call(bf16[1024,1728]{1,0:T(8,128)(2,1)S(1)} %add_convert_fusion.packed_ref.refs_0_), custom_call_target="tpu_custom_call" | custom-call | flops 4294967296 | bytes 4128768 | tf_op jit(solution)/shard_map/pallas_call | solution.py:79
  101.6 18.2 %collective-permute-done.3 = bf16[512,1152]{1,0:T(8,128)(2,1)S(1)} collective-permute-done((bf16[512,1152]{1,0:T(8,128)(2,1)}, bf16[512,1152]{1,0:T(8,128)(2,1)S(1)}, u32[]{:S(2)}, u32[]{:S(2)}) %collective-permute-start.3) | collective-permute-done | bytes 1179680 | tf_op jit(solution)/shard_map/ppermute | solution.py:300
  129.5 22.2 %collective-permute-done.4 = bf16[512,1152]{1,0:T(8,128)(2,1)S(1)} collective-permute-done((bf16[512,1152]{1,0:T(8,128)(2,1)S(1)}, bf16[512,1152]{1,0:T(8,128)(2,1)S(1)}, u32[]{:S(2)}, u32[]{:S(2)}) %collective-permute-start.4) | collective-permute-done | bytes 1179680 | tf_op jit(solution)/shard_map/ppermute | solution.py:300
  153.2 10.6 %all-gather.5.cloned.1.call-done.up_ref.down_ref = bf16[1152,4608]{1,0:T(8,128)(2,1)} async-done(((bf16[72,4608]{1,0:T(8,128)(2,1)}), bf16[1152,4608]{1,0:T(8,128)(2,1)}) %all-gather.5.cloned.1.call-update) | async-done | bytes 10616848 | tf_op jit(solution)/shard_map/all_gather | solution.py:407
  167.2 16.3 %shard_map.230 = (bf16[1024,2304]{1,0:T(8,128)(2,1)}, bf16[1024,2304]{1,0:T(8,128)(2,1)}, f32[1,2304]{1,0:T(1,128)S(1)}) custom-call(bf16[1024,1152]{1,0:T(8,128)(2,1)S(1)} %copy-done.1, bf16[1024,1152]{1,0:T(8,128)(2,1)S(1)} %copy-done, bf16[1152,4608]{1,0:T(8,128)(2,1)} %all-gather.5.cloned.1.call-done.up_ref.down_ref, ...), custom_call_target="tpu_custom_call" | custom-call | flops 10871635968 | bytes 24772608 | tf_op jit(solution)/shard_map/pallas_call | solution.py:193
  183.5 17.0 %shard_map.231 = bf16[1152,4608]{1,0:T(8,128)(2,1)} custom-call(bf16[1024,1152]{1,0:T(8,128)(2,1)S(1)} %copy-done, bf16[1024,1152]{1,0:T(8,128)(2,1)S(1)} %copy-done.1, bf16[1024,2304]{1,0:T(8,128)(2,1)} %get-tuple-element.65.act_ref, bf16[1024,2304]{1,0:T(8,128)(2,1)} %get-tuple-element.66.pre_ref), custom_call_target="tpu_custom_call" | custom-call | flops 10871635968 | bytes 24772608 | tf_op jit(solution)/shard_map/pallas_call | solution.py:247
  203.7 8.2 %fusion.22 = bf16[512,1152]{1,0:T(8,128)(2,1)S(1)} fusion(bf16[1152,4608]{1,0:T(8,128)(2,1)} %all-gather.5.cloned.1.call-done.up_ref.down_ref, bf16[1024,2304]{1,0:T(8,128)(2,1)} %get-tuple-element.66.pre_ref), kind=kOutput, calls=%fused_computation.27 | convolution fusion | flops 2718498816 | bytes 8847360 | tf_op jit(solution)/shard_map/dot_general | solution.py:23
  213.6 4.3 %fusion.19 = bf16[512,1152]{1,0:T(8,128)(2,1)} fusion(bf16[1152,4608]{1,0:T(8,128)(2,1)S(1)} %bitcast.45, bf16[1024,2304]{1,0:T(8,128)(2,1)S(1)} %bitcast.47), kind=kOutput, calls=%fused_computation.26 | convolution fusion | flops 2718498816 | bytes 8847360 | tf_op jit(solution)/shard_map/dot_general | solution.py:23
  217.8 4.6 %fusion.12 = f32[512,1152]{1,0:T(8,128)} fusion(bf16[1152,4608]{1,0:T(8,128)(2,1)S(1)} %bitcast.45, bf16[1024,2304]{1,0:T(8,128)(2,1)S(1)} %bitcast.47), kind=kOutput, calls=%fused_computation.15 | convolution fusion | flops 2717908992 | bytes 10027008 | tf_op jit(solution)/shard_map/dot_general | solution.py:23
  222.5 17.7 %collective-permute-done.5 = bf16[512,1152]{1,0:T(8,128)(2,1)S(1)} collective-permute-done((bf16[512,1152]{1,0:T(8,128)(2,1)S(1)}, bf16[512,1152]{1,0:T(8,128)(2,1)S(1)}, u32[]{:S(2)}, u32[]{:S(2)}) %collective-permute-start.5) | collective-permute-done | bytes 1179680 | tf_op jit(solution)/shard_map/ppermute | solution.py:300
  240.2 5.4 %multiply_reduce_fusion = (f32[1152]{0:T(1024)S(1)}, f32[512]{0:T(512)S(1)}, f32[512]{0:T(512)S(1)}, f32[1152]{0:T(1024)S(1)}, f32[512,1152]{1,0:T(8,128)S(1)}) fusion(f32[512,1152]{1,0:T(8,128)S(1)} %copy-done.16, f32[512]{0:T(512)S(1)} %add_rsqrt_fusion.2, f32[512]{0:T(512)S(1)} %broadcast_multiply_fusion.6, f32[1152]{0:T(1024)S(1)} %copy-done.31, ...), kind=kOutput, calls=%fused_computation.49 | convolution fusion | flops 2724393984 | bytes 13591552 | tf_op jit(solution)/shard_map/dot_general | solution.py:23
  245.6 3.1 multiply_reduce_fusion.1
  252.9 4.1 convolution_convert_fusion.1
  261.4 14.4 %shard_map.232 = (bf16[512,576]{1,0:T(8,128)(2,1)S(1)}, f32[1024,576]{1,0:T(8,128)S(1)}, f32[1024,576]{1,0:T(8,128)}) custom-call(bf16[1024,1728]{1,0:T(8,128)(2,1)} %copy-done.7, bf16[512,576]{1,0:T(8,128)(2,1)S(1)} %copy-done.5, bf16[512,576]{1,0:T(8,128)(2,1)S(1)} %copy-done.4, f32[8,512]{1,0:T(8,128)S(1)} %get-tuple-element.69.refs_3_), custom_call_target="tpu_custom_call" | custom-call | flops 10737418240 | bytes 10027008 | tf_op jit(solution)/shard_map/pallas_call | solution.py:158
  280.6 4.1 convolution_convert_fusion.2
  289.8 16.3 %shard_map.233 = (bf16[1024,1728]{1,0:T(8,128)(2,1)}, f32[1,1728]{1,0:T(1,128)S(1)}) custom-call(bf16[1024,1728]{1,0:T(8,128)(2,1)} %copy-done.7, bf16[512,576]{1,0:T(8,128)(2,1)S(1)} %copy-done.6, bf16[512,576]{1,0:T(8,128)(2,1)S(1)} %get-tuple-element.59.refs_2_, f32[8,512]{1,0:T(8,128)S(1)} %get-tuple-element.68.refs_3_, bf16[512,576]{1,0:T(8,128)(2,1)S(1)} %copy-done.11, ...), custom_call_target="tpu_custom_call" | custom-call | flops 10737418240 | bytes 10027008 | tf_op jit(solution)/shard_map/pallas_call | solution.py:158
  306.0 11.4 %shard_map.234 = bf16[1152,2304]{1,0:T(8,128)(2,1)} custom-call(bf16[1024,1152]{1,0:T(8,128)(2,1)S(1)} %fusion.5.first_ref, bf16[1024,1728]{1,0:T(8,128)(2,1)} %get-tuple-element.76.packed_ref, bf16[1024,1152]{1,0:T(8,128)(2,1)S(1)} %pad_maximum_fusion.3.upstream_ref, bf16[1024,576]{1,0:T(8,128)(2,1)S(1)} %copy-done.2), custom_call_target="tpu_custom_call" | custom-call | flops 5435817984 | bytes 14745600 | tf_op jit(solution)/shard_map/pallas_call | solution.py:285
  317.5 3.8 add_add_fusion
  321.3 10.4 %fusion.6 = (f32[1152]{0:T(1024)S(1)}, f32[1152]{0:T(1024)S(1)}, f32[1024,1152]{1,0:T(8,128)}) fusion(f32[1024]{0:T(1024)S(1)} %copy-done.42, f32[1024]{0:T(1024)S(1)} %copy-done.33, bf16[512,1152]{1,0:T(8,128)(2,1)S(1)} %copy-done.20, bf16[512,1152]{1,0:T(8,128)(2,1)S(1)} %copy-done.14, bf16[1024,1728]{1,0:T(8,128)(2,1)} %get-tuple-element.76.packed_ref, ...), kind=kOutput, calls=%fused_computation.9 | convolution fusion | flops 4087478272 | bytes 14894080 | tf_op jit(solution)/shard_map/dot_general | solution.py:23
  334.1 4.4 %fusion.34 = (f32[1152]{0:T(1024)S(1)}, bf16[512,1152]{1,0:T(8,128)(2,1)}) fusion(f32[512,1152]{1,0:T(8,128)} %add_add_fusion, bf16[512,1152]{1,0:T(8,128)(2,1)} %param.25, f32[512,1152]{1,0:T(8,128)} %copy-done.15, f32[1152]{0:T(1024)S(1)} %get-tuple-element.162), kind=kLoop, calls=%fused_computation.40 | loop fusion | flops 3537792 | bytes 7087104 | tf_op jit(solution)/shard_map/reduce_sum | solution.py:428
  339.2 3.4 collective-permute-done.8
  346.6 3.6 all-to-all-start.2
  350.8 16.8 %all-to-all-done.2 = f32[16,1,9792]{2,1,0:T(1,128)S(1)} async-done(((f32[16,1,9792]{2,1,0:T(1,128)}), f32[16,1,9792]{2,1,0:T(1,128)S(1)}, u32[]{:S(2)}, u32[]{:S(2)}) %all-to-all-start.2) | async-done | bytes 626720 | tf_op jit(solution)/shard_map/all_to_all | solution.py:339
  384.3 11.0 %all-to-all-start.3 = ((f32[16,1,72]{2,1,0:T(1,128)}), f32[16,1,72]{2,1,0:T(1,128)S(1)}, u32[]{:S(2)}, u32[]{:S(2)}) async-start(f32[16,1,72]{2,1,0:T(1,128)} %bitcast.6), calls=%async_computation.3 | async-start | bytes 16384 | tf_op jit(solution)/shard_map/all_to_all | solution.py:339
  398.1 3.7 all-to-all-done.3
  406.8 5.8 %reduce-scatter.5.cloned.1.call-done = bf16[72,2304]{1,0:T(8,128)(2,1)} async-done(((bf16[1152,2304]{1,0:T(8,128)(2,1)}), bf16[72,2304]{1,0:T(8,128)(2,1)}) %reduce-scatter.5.cloned.1.call-update) | async-done | bytes 331792 | tf_op jit(solution)/shard_map/reduce_scatter | solution.py:475
  (232 shorter events, 96.7 us)
Async XLA Ops:
  7.2 14.2 %copy-start.28 = (bf16[72,6,576]{2,0,1:T(8,128)(2,1)S(1)}, bf16[72,6,576]{2,0,1:T(8,128)(2,1)}, u32[]{:S(2)}) copy-start(bf16[72,6,576]{2,0,1:T(8,128)(2,1)} %param.15) | copy-start | bytes 1492996
  7.2 66.5 %all-gather.3.cloned.1.call-start = ((), (), s32[]{:S(2)}) async-start(), calls=%async_computation.6 | async-start | bytes 5640192 | tf_op jit(solution)/shard_map/all_gather | solution.py:390
  10.4 31.3 %collective-permute-start = (bf16[512,1152]{1,0:T(8,128)(2,1)}, bf16[512,1152]{1,0:T(8,128)(2,1)S(1)}, u32[]{:S(2)}, u32[]{:S(2)}) collective-permute-start(bf16[512,1152]{1,0:T(8,128)(2,1)} %param.13), channel_id=1, source_target_pairs={{0,1},{1,0},{2,3},{3,2},{4,5},{5,4},{6,7},{7,6},{8,9},{9,8},{10,11... | collective-permute-start | bytes 3538952 | tf_op jit(solution)/shard_map/ppermute | solution.py:300
  15.4 12.3 %all-to-all-start = ((bf16[16,1,72]{2,1,0:T(2,128)(2,1)}), bf16[16,1,72]{2,1,0:T(2,128)(2,1)S(1)}, u32[]{:S(2)}, u32[]{:S(2)}) async-start(bf16[16,1,72]{2,1,0:T(2,128)(2,1)} %transpose_reshape.4), calls=%async_computation | async-start | bytes 16384 | tf_op jit(solution)/shard_map/all_to_all | solution.py:339
  21.3 142.5 %all-gather.5.cloned.1.call-start = ((), (), s32[]{:S(2)}) async-start(), calls=%async_computation.7 | async-start | bytes 11280384 | tf_op jit(solution)/shard_map/all_gather | solution.py:407
  22.0 26.9 %copy-start.21 = (bf16[72,3456]{1,0:T(8,128)(2,1)}, bf16[72,3456]{1,0:T(8,128)(2,1)S(1)}, u32[]{:S(2)}) copy-start(bf16[72,3456]{1,0:T(8,128)(2,1)S(1)} %reshape.166) | copy-start | bytes 1492996
  22.0 24.3 %copy-start.46 = (bf16[2,576]{1,0:T(2,128)(2,1)S(1)}, bf16[2,576]{1,0:T(2,128)(2,1)}, u32[]{:S(2)}) copy-start(bf16[2,576]{1,0:T(2,128)(2,1)} %param.18) | copy-start | bytes 6916
  22.0 26.5 %copy-start.12 = (bf16[512,1152]{1,0:T(8,128)(2,1)S(1)}, bf16[512,1152]{1,0:T(8,128)(2,1)}, u32[]{:S(2)}) copy-start(bf16[512,1152]{1,0:T(8,128)(2,1)} %param.13) | copy-start | bytes 3538948
  27.7 21.2 %copy-start.36 = (bf16[16,1,72]{2,1,0:T(2,128)(2,1)}, bf16[16,1,72]{2,1,0:T(2,128)(2,1)S(1)}, u32[]{:S(2)}) copy-start(bf16[16,1,72]{2,1,0:T(2,128)(2,1)S(1)} %all-to-all-done) | copy-start | bytes 6916
  42.4 3.8 collective-permute-start.1
  46.3 285.5 %reduce-scatter.3.cloned.1.call-start = ((), (), s32[]{:S(2)}) async-start(), calls=%async_computation.8 | async-start | bytes 11280384 | tf_op jit(solution)/shard_map/reduce_scatter | solution.py:475
  47.0 34.2 %collective-permute-start.2 = (bf16[512,1152]{1,0:T(8,128)(2,1)}, bf16[512,1152]{1,0:T(8,128)(2,1)}, u32[]{:S(2)}, u32[]{:S(2)}) collective-permute-start(bf16[512,1152]{1,0:T(8,128)(2,1)} %param.25), channel_id=1, source_target_pairs={{0,1},{1,0},{2,3},{3,2},{4,5},{5,4},{6,7},{7,6},{8,9},{9,8},{10,11... | collective-permute-start | bytes 3538952 | tf_op jit(solution)/shard_map/ppermute | solution.py:300
  91.5 28.3 %collective-permute-start.3 = (bf16[512,1152]{1,0:T(8,128)(2,1)}, bf16[512,1152]{1,0:T(8,128)(2,1)S(1)}, u32[]{:S(2)}, u32[]{:S(2)}) collective-permute-start(bf16[512,1152]{1,0:T(8,128)(2,1)} %convolution_convert_fusion), channel_id=1, source_target_pairs={{0,1},{1,0},{2,3},{3,2},{4,5},{5,4},{6,7},{7,6},{8,9},{9,8},{10,11... | collective-permute-start | bytes 3538952 | tf_op jit(solution)/shard_map/ppermute | solution.py:300
  93.2 26.6 %copy-start.38 = (f32[512]{0:T(512)}, f32[512]{0:T(512)S(1)}, u32[]{:S(2)}) copy-start(f32[512]{0:T(512)S(1)} %broadcast_multiply_fusion.3) | copy-start | bytes 6148
  93.2 26.6 %copy-start.34 = (f32[1152]{0:T(1024)S(1)}, f32[1152]{0:T(1024)}, u32[]{:S(2)}) copy-start(f32[1152]{0:T(1024)} %get-tuple-element.165) | copy-start | bytes 13828
  101.6 21.2 %copy-start.3 = (bf16[512,576]{1,0:T(8,128)(2,1)}, bf16[512,576]{1,0:T(8,128)(2,1)S(1)}, u32[]{:S(2)}) copy-start(bf16[512,576]{1,0:T(8,128)(2,1)S(1)} %get-tuple-element.58.refs_2_) | copy-start | bytes 1769476
  124.2 27.4 %collective-permute-start.4 = (bf16[512,1152]{1,0:T(8,128)(2,1)S(1)}, bf16[512,1152]{1,0:T(8,128)(2,1)S(1)}, u32[]{:S(2)}, u32[]{:S(2)}) collective-permute-start(bf16[512,1152]{1,0:T(8,128)(2,1)S(1)} %add_convert_fusion.2), channel_id=1, source_target_pairs={{0,1},{1,0},{2,3},{3,2},{4,5},{5,4},{6,7},{7,6},{8,9},{9,8},{10,11... | collective-permute-start | bytes 3538952 | tf_op jit(solution)/shard_map/ppermute | solution.py:300
  200.6 212.0 %reduce-scatter.5.cloned.1.call-start = ((), (), s32[]{:S(2)}) async-start(), calls=%async_computation.9 | async-start | bytes 5640192 | tf_op jit(solution)/shard_map/reduce_scatter | solution.py:475
  201.3 12.3 %slice-start = ((s8[10616832]{0:T(1024)(128)(4,1)}), s8[4194304]{0:T(1024)(128)(4,1)S(1)}, s32[]{:S(2)}) async-start(s8[10616832]{0:T(1024)(128)(4,1)} %bitcast.44), calls=%async_computation.10 | async-start | bytes 8388608
  201.3 12.3 %slice-start.3 = ((s8[4718592]{0:T(1024)(128)(4,1)}), s8[4194304]{0:T(1024)(128)(4,1)S(1)}, s32[]{:S(2)}) async-start(s8[4718592]{0:T(1024)(128)(4,1)} %bitcast.46), calls=%async_computation.13 | async-start | bytes 8388608
  211.9 28.2 %collective-permute-start.5 = (bf16[512,1152]{1,0:T(8,128)(2,1)S(1)}, bf16[512,1152]{1,0:T(8,128)(2,1)S(1)}, u32[]{:S(2)}, u32[]{:S(2)}) collective-permute-start(bf16[512,1152]{1,0:T(8,128)(2,1)S(1)} %fusion.22), channel_id=1, source_target_pairs={{0,1},{1,0},{2,3},{3,2},{4,5},{5,4},{6,7},{7,6},{8,9},{9,8},{10,11... | collective-permute-start | bytes 3538952 | tf_op jit(solution)/shard_map/ppermute | solution.py:300
  217.8 22.4 %copy-start.16 = (f32[512,1152]{1,0:T(8,128)S(1)}, f32[512,1152]{1,0:T(8,128)}, u32[]{:S(2)}) copy-start(f32[512,1152]{1,0:T(8,128)} %copy-done.15) | copy-start | bytes 7077892
  222.5 23.1 %copy-start.24 = (f32[512,1152]{1,0:T(8,128)S(1)}, f32[512,1152]{1,0:T(8,128)}, u32[]{:S(2)}) copy-start(f32[512,1152]{1,0:T(8,128)} %get-tuple-element.190) | copy-start | bytes 7077892
  222.5 23.1 %copy-start.27 = (bf16[512,1152]{1,0:T(8,128)(2,1)S(1)}, bf16[512,1152]{1,0:T(8,128)(2,1)}, u32[]{:S(2)}) copy-start(bf16[512,1152]{1,0:T(8,128)(2,1)} %copy-done.26) | copy-start | bytes 3538948
  251.4 27.8 %collective-permute-start.6 = (bf16[512,1152]{1,0:T(8,128)(2,1)}, bf16[512,1152]{1,0:T(8,128)(2,1)}, u32[]{:S(2)}, u32[]{:S(2)}) collective-permute-start(bf16[512,1152]{1,0:T(8,128)(2,1)} %get-tuple-element.171), channel_id=1, source_target_pairs={{0,1},{1,0},{2,3},{3,2},{4,5},{5,4},{6,7},{7,6},{8,9},{9,8},{10,11... | collective-permute-start | bytes 3538952 | tf_op jit(solution)/shard_map/ppermute | solution.py:300
  279.2 38.3 %collective-permute-start.7 = (bf16[512,1152]{1,0:T(8,128)(2,1)}, bf16[512,1152]{1,0:T(8,128)(2,1)}, u32[]{:S(2)}, u32[]{:S(2)}) collective-permute-start(bf16[512,1152]{1,0:T(8,128)(2,1)} %fusion.19), channel_id=1, source_target_pairs={{0,1},{1,0},{2,3},{3,2},{4,5},{5,4},{6,7},{7,6},{8,9},{9,8},{10,11... | collective-permute-start | bytes 3538952 | tf_op jit(solution)/shard_map/ppermute | solution.py:300
  289.8 16.3 %copy-start.2 = (bf16[1024,576]{1,0:T(8,128)(2,1)S(1)}, bf16[1024,576]{1,0:T(8,128)(2,1)}, u32[]{:S(2)}) copy-start(bf16[1024,576]{1,0:T(8,128)(2,1)} %pad_maximum_fusion.4.heads_ref) | copy-start | bytes 3538948
  338.5 4.0 collective-permute-start.8
  344.5 25.3 %collective-permute-start.9 = (bf16[512,1152]{1,0:T(8,128)(2,1)S(1)}, bf16[512,1152]{1,0:T(8,128)(2,1)}, u32[]{:S(2)}, u32[]{:S(2)}) collective-permute-start(bf16[512,1152]{1,0:T(8,128)(2,1)S(1)} %slice.221), channel_id=1, source_target_pairs={{0,1},{1,0},{2,3},{3,2},{4,5},{5,4},{6,7},{7,6},{8,9},{9,8},{10,11... | collective-permute-start | bytes 3538952 | tf_op jit(solution)/shard_map/ppermute | solution.py:300
  346.6 21.0 %all-to-all-start.2 = ((f32[16,1,9792]{2,1,0:T(1,128)}), f32[16,1,9792]{2,1,0:T(1,128)S(1)}, u32[]{:S(2)}, u32[]{:S(2)}) async-start(f32[16,1,9792]{2,1,0:T(1,128)} %broadcast_in_dim.45), calls=%async_computation.2 | async-start | bytes 1261568 | tf_op jit(solution)/shard_map/all_to_all | solution.py:339
  372.4 10.7 %collective-permute-start.10 = (f32[16,72]{1,0:T(8,128)S(1)}, f32[16,72]{1,0:T(8,128)}, u32[]{:S(2)}, u32[]{:S(2)}) collective-permute-start(f32[16,72]{1,0:T(8,128)S(1)} %fusion.56), channel_id=1, source_target_pairs={{0,1},{1,0},{2,3},{3,2},{4,5},{5,4},{6,7},{7,6},{8,9},{9,8},{10,11... | collective-permute-start | bytes 13832 | tf_op jit(solution)/shard_map/ppermute | solution.py:300
  384.3 17.4 %all-to-all-start.3 = ((f32[16,1,72]{2,1,0:T(1,128)}), f32[16,1,72]{2,1,0:T(1,128)S(1)}, u32[]{:S(2)}, u32[]{:S(2)}) async-start(f32[16,1,72]{2,1,0:T(1,128)} %bitcast.6), calls=%async_computation.3 | async-start | bytes 16384 | tf_op jit(solution)/shard_map/all_to_all | solution.py:339
  (39 other events, 139.8 us)
Sparse Core Ops, SparseCore 0:
  10.8 62.9 all-gather.2
  76.6 87.2 all-gather.4
  200.7 118.3 reduce-scatter.2
  334.2 78.3 reduce-scatter.4

commit v3 on v2

--- a/solution.py
+++ b/solution.py
@@ -94,12 +94,14 @@
 
 
 def attend_back_kernel(start, last, *refs):
-    packed_ref, up_ref, heads_ref, log_ref = refs[:4]
+    packed_ref, upstream_ref, weight_ref, heads_ref, log_ref = refs[:5]
+    up_ref = refs[-1]
     rows, cols = up_ref.shape
     if last:
-        query_ins, key_in, value_in, out_ref, sum_ref = refs[4:-4], *refs[-4:]
+        query_ins, key_in, value_in, out_ref, sum_ref = refs[5:-5], *refs[-5:-1]
     else:
-        query_ref, key_ref, value_ref = refs[4:]
+        query_ref, key_ref, value_ref = refs[5:-1]
+    up_ref[...] = mm(upstream_ref[...], weight_ref[...]).astype(jnp.bfloat16)
     scale = 1.0 / math.sqrt(HD)
     factor = LOG2E * scale
     products = (up_ref[...].astype(jnp.float32) * heads_ref[...].astype(jnp.float32)).T
@@ -137,12 +139,12 @@
         query_ref[...] = query_grad
 
 
-def attend_back(packed, start, upstream, heads_low, logs, query_grads, sums, last):
+def attend_back(packed, start, upstream, weight, heads_low, logs, query_grads, sums, last):
     length, width = packed.shape
     cols = width // 3
     heads = cols // HD
     rows = upstream.shape[0]
-    operands = (packed, upstream, heads_low, logs)
+    operands = (packed, upstream, weight, heads_low, logs)
     if last:
         operands += tuple(query_grads) + tuple(sums)
         shapes = (
@@ -160,6 +162,7 @@
         out_shape=shapes,
         in_specs=[pl.BlockSpec(memory_space=pltpu.VMEM)] * len(operands),
         out_specs=jax.tree.map(lambda _: pl.BlockSpec(memory_space=pltpu.VMEM), shapes),
+        scratch_shapes=[pltpu.VMEM((rows, cols), jnp.bfloat16)],
         compiler_params=pltpu.CompilerParams(vmem_limit_bytes=VMEM_LIMIT),
         cost_estimate=pl.CostEstimate(
             flops=10 * rows * length * 256 * heads,
@@ -215,24 +218,16 @@
     )(second, feed_grad, weights, weights, bias)
 
 
-def feed_weight_kernel(tiles, feed_ref, second_ref, act_ref, pre_ref, out_ref, turned_ref):
+def feed_weight_kernel(tiles, feed_ref, second_ref, act_ref, pre_ref, out_ref):
     step = pl.program_id(0)
-
-    @pl.when(step == 0)
-    def _():
-        turned_ref[...] = feed_ref[...].T
-
-    @pl.when(step == tiles)
-    def _():
-        turned_ref[...] = second_ref[...].T
 
     @pl.when(step < tiles)
     def _():
-        out_ref[...] = mm(turned_ref[...], act_ref[...]).astype(jnp.bfloat16)
+        out_ref[...] = mm(feed_ref[...], act_ref[...], BOTH_FIRST).astype(jnp.bfloat16)
 
     @pl.when(step >= tiles)
     def _():
-        out_ref[...] = mm(turned_ref[...], pre_ref[...]).astype(jnp.bfloat16)
+        out_ref[...] = mm(second_ref[...], pre_ref[...], BOTH_FIRST).astype(jnp.bfloat16)
 
 
 def feed_weight_grads(feed_grad, second, act, pre):
@@ -255,7 +250,6 @@
             pl.BlockSpec((rows, tile), lambda j: (0, jnp.maximum(j - tiles, 0))),
         ],
         out_specs=pl.BlockSpec((width, tile), lambda j: (0, j)),
-        scratch_shapes=[pltpu.VMEM((width, rows), jnp.bfloat16)],
         compiler_params=pltpu.CompilerParams(vmem_limit_bytes=VMEM_LIMIT),
         cost_estimate=pl.CostEstimate(
             flops=4 * rows * width * hidden,
@@ -333,6 +327,11 @@
     if lax.axis_size("tp") == 2:
         return values + swap(values)
     return lax.psum(values, "tp")
+
+
+def gather_blocks(shard):
+    whole = lax.all_gather(shard[None], "fsdp", axis=0, tiled=True)
+    return whole.reshape(-1, shard.shape[1])
 
 
 def exchange(blocks):
@@ -387,7 +386,7 @@
     bf16 = jnp.bfloat16
 
     first_shard = jnp.concatenate([attention_weight.reshape(depth, 3 * cols), output_weight.T], axis=1)
-    first_weights = lax.all_gather(first_shard, "fsdp", axis=0, tiled=True)
+    first_weights = gather_blocks(first_shard)
     attention_all = first_weights[:, : 3 * cols]
     output_all = first_weights[:, 3 * cols :]
     feed_shard = jnp.concatenate([up_weight, down_weight.T], axis=1)
@@ -404,7 +403,7 @@
     own_columns, inputs_parts = lax.optimization_barrier((own_columns, inputs_parts))
     modulation = gather_columns(own_columns + modulation_bias.astype(f32))
     feed_shard, modulation = lax.optimization_barrier((feed_shard, modulation))
-    feed_weights = lax.all_gather(feed_shard, "fsdp", axis=0, tiled=True)
+    feed_weights = gather_blocks(feed_shard)
     up_all = feed_weights[:, :hidden]
     down_all = feed_weights[:, hidden:]
     own_modulation = modulation[0]
@@ -495,11 +494,11 @@
         feed_sums[1] = feed_sums[1].astype(bf16)
         feed_sums[1], upstream_parts[1] = lax.optimization_barrier((feed_sums[1], upstream_parts[1]))
     feed = scatter_rows(feed_sums, paired) + down_bias.astype(f32)
-    if paired:
-        heads_grads = [mm(part, output_all).astype(bf16) for part in upstream_parts]
-    else:
-        heads_grad = mm(upstream_parts[0], output_all).astype(bf16)
-        heads_grads = [heads_grad[n * block : (n + 1) * block] for n in range(group_blocks)]
+    heads_upstream = upstream_parts
+    if not paired:
+        heads_upstream = [
+            upstream_parts[0][n * block : (n + 1) * block] for n in range(group_blocks)
+        ]
     packed_parts = []
     packed_sums = []
     for latent in range(latents):
@@ -510,7 +509,8 @@
             result = attend_back(
                 packed_latents[latent],
                 step * block,
-                heads_grads[at],
+                heads_upstream[at],
+                output_all,
                 heads_parts[at],
                 logs[at],
                 query_grads,
@@ -535,7 +535,6 @@
     first_grads = scatter_weights(first_grads)
     grad_attention = first_grads[:, : 3 * cols]
     grad_output = first_grads[:, 3 * cols :].T
-    outputs = (mid + own_rows(5) * feed).astype(bf16)
     first_grad_all = mm(packed_low, attention_all, BOTH_LAST)
 
     own_feed = feed_parts[0]
@@ -576,7 +575,10 @@
         ]
     )
     shared = share(sums[None]).reshape(fsdp, -1)
-    shared, first_grad = lax.optimization_barrier((shared, first_grad))
+    shared, first_grad, feed, feed_grads = lax.optimization_barrier(
+        (shared, first_grad, feed, feed_grads)
+    )
+    outputs = (mid + own_rows(5) * feed).astype(bf16)
     modulation_all = shared[:, : latents * 6 * cols].reshape(fsdp * latents, 6 * cols).astype(bf16)
     bias_sums = jnp.sum(shared[:, latents * 6 * cols :], axis=0)
     grad_modulation_weight = mm(silu_rows, modulation_all, BOTH_FIRST).reshape(depth, 6, cols)

time: 429 us -> 418 us (0.974)
  waiting for transfers between devices: 129 us -> 139 us
  other arithmetic: 48.4 us -> 39 us
  local copies, waits for them, and re-layouts: 33.8 us -> 24.6 us
    reduce_scatter x2, waiting for transfers between devices: 5.84 us -> 16.5 us  [scatter_weights(): lax.psum_scatter(values.astype(bf16), 'fsdp', scatter_dimension=0, tiled=...]
    unnamed x110 -> x98, local copies, waits for them, and re-layouts: 13.5 us -> 6.48 us
    all_to_all x3, starting transfers between devices: 20.5 us -> 15.2 us  [exchange(): return lax.all_to_all(blocks, 'fsdp', 0, 0, tiled=True)]
    dot_general x13 -> x11, matrix products: 55.6 us -> 53 us  [mm(): return lax.dot_general(a, b, dims, preferred_element_type=jnp.float32)]
  transfers between devices with their start and end apart: 18 -> 18, of which waited for: 13 -> 14; matrix products, arithmetic and copies ran while one was open for 28% -> 25% of each run, Pallas kernels for 14% -> 15%
where the time goes in v3:
time: 418 us; the launch traced here: 411 us
  waiting for transfers between devices  139 us (33%)
  Pallas kernels  94.6 us (23%)
  matrix products  53 us (13%)
  other arithmetic  39 us (9%)
  starting transfers between devices  33.2 us (8%)
  local copies, waits for them, and re-layouts  24.6 us (6%)
  between operations  14.8 us (4%)
  blocking collectives  13.3 us (3%)
    ppermute x11, waiting for transfers between devices, swap(): return lax.ppermute(values, 'tp', [(0, 1), (1, 0)])  65.2 us
    dot_general x11, matrix products, mm(): return lax.dot_general(a, b, dims, preferred_element_type=jnp.float32)  53 us
    pallas_call x2, Pallas kernels, attend_back(): pl.pallas_call(functools.partial(attend_back_kernel, start, last), out_sh...  34.7 us
    all_gather x2, waiting for transfers between devices, gather_blocks(): whole = lax.all_gather(shard[None], 'fsdp', axis=0, tiled=True)  31.8 us
    all_to_all x3, waiting for transfers between devices, exchange(): return lax.all_to_all(blocks, 'fsdp', 0, 0, tiled=True)  24.9 us
    ppermute x11, starting transfers between devices, swap(): return lax.ppermute(values, 'tp', [(0, 1), (1, 0)])  17.9 us
    reduce_scatter x2, waiting for transfers between devices, scatter_weights(): lax.psum_scatter(values.astype(bf16), 'fsdp', scatter_dimension=0, tiled=...  16.5 us
    pallas_call x1, Pallas kernels, feed_forward(): pl.pallas_call(feed_kernel, grid=(tiles,), out_shape=(jax.ShapeDtypeStruc...  16.3 us
  transfers between devices with their start and end apart: 18, of which 14 were waited for; matrix products, arithmetic and copies ran while one was open for 25% of the time, Pallas kernels for 15%

profile of v3, /device:TPU:0, one launch (start us, length us, event | category | flops | bytes accessed | tf_op | source)
XLA Modules:
  0.0 411.2 jit_solution(11471253531614018800)
XLA Ops:
  10.4 3.0 collective-permute-start
  15.4 5.9 %all-to-all-start = ((bf16[16,1,72]{2,1,0:T(2,128)(2,1)}), bf16[16,1,72]{2,1,0:T(2,128)(2,1)S(1)}, u32[]{:S(2)}, u32[]{:S(2)}) async-start(bf16[16,1,72]{2,1,0:T(2,128)(2,1)} %transpose_reshape.4), calls=%async_computation | async-start | bytes 16384 | tf_op jit(solution)/shard_map/all_to_all | solution.py:338
  22.0 5.7 %all-to-all-done = bf16[16,1,72]{2,1,0:T(2,128)(2,1)S(1)} async-done(((bf16[16,1,72]{2,1,0:T(2,128)(2,1)}), bf16[16,1,72]{2,1,0:T(2,128)(2,1)S(1)}, u32[]{:S(2)}, u32[]{:S(2)}) %all-to-all-start) | async-done | bytes 2336 | tf_op jit(solution)/shard_map/all_to_all | solution.py:338
  28.1 13.3 %all_to_all.20 = f32[16,1,3456]{2,1,0:T(1,128)S(1)} all-to-all(f32[16,1,3456]{2,1,0:T(1,128)S(1)} %copy.43), channel_id=1, replica_groups=mesh['fsdp'=16,'tp'=2] {'fsdp'}, dimensions={0} | all-to-all | bytes 442368 | tf_op jit(solution)/shard_map/all_to_all | solution.py:338
  52.5 21.2 %all-gather.5.cloned.1.call-done = bf16[1152,2304]{1,0:T(8,128)(2,1)} async-done(((bf16[72,2304]{1,0:T(8,128)(2,1)}), bf16[1152,2304]{1,0:T(8,128)(2,1)}) %all-gather.5.cloned.1.call-update) | async-done | bytes 5308432 | tf_op jit(solution)/shard_map/all_gather | solution.py:333
  73.7 7.4 %add_convert_fusion.packed_ref.refs_0_ = bf16[1024,1728]{1,0:T(8,128)(2,1)S(1)} fusion(bf16[1024,1152]{1,0:T(8,128)(2,1)S(1)} %fusion.5.first_ref, f32[1728]{0:T(1024)} %concatenate.37, bf16[1152,2304]{1,0:T(8,128)(2,1)} %all-gather.5.cloned.1.call-done), kind=kOutput, calls=%fused_computation | convolution fusion | flops 4080402432 | bytes 10035200 | tf_op jit(solution)/shard_map/dot_general | solution.py:23
  81.2 7.9 %shard_map.229 = (bf16[512,576]{1,0:T(8,128)(2,1)S(1)}, f32[8,512]{1,0:T(8,128)S(1)}) custom-call(bf16[1024,1728]{1,0:T(8,128)(2,1)S(1)} %add_convert_fusion.packed_ref.refs_0_), custom_call_target="tpu_custom_call" | custom-call | flops 4294967296 | bytes 4128768 | tf_op jit(solution)/shard_map/pallas_call | solution.py:79
  93.2 8.2 %shard_map.228 = (bf16[512,576]{1,0:T(8,128)(2,1)S(1)}, f32[8,512]{1,0:T(8,128)S(1)}) custom-call(bf16[1024,1728]{1,0:T(8,128)(2,1)S(1)} %add_convert_fusion.packed_ref.refs_0_), custom_call_target="tpu_custom_call" | custom-call | flops 4294967296 | bytes 4128768 | tf_op jit(solution)/shard_map/pallas_call | solution.py:79
  101.4 18.4 %collective-permute-done.3 = bf16[512,1152]{1,0:T(8,128)(2,1)S(1)} collective-permute-done((bf16[512,1152]{1,0:T(8,128)(2,1)}, bf16[512,1152]{1,0:T(8,128)(2,1)S(1)}, u32[]{:S(2)}, u32[]{:S(2)}) %collective-permute-start.3) | collective-permute-done | bytes 1179680 | tf_op jit(solution)/shard_map/ppermute | solution.py:294
  119.9 3.0 fusion.55
  129.5 22.2 %collective-permute-done.4 = bf16[512,1152]{1,0:T(8,128)(2,1)S(1)} collective-permute-done((bf16[512,1152]{1,0:T(8,128)(2,1)S(1)}, bf16[512,1152]{1,0:T(8,128)(2,1)S(1)}, u32[]{:S(2)}, u32[]{:S(2)}) %collective-permute-start.4) | collective-permute-done | bytes 1179680 | tf_op jit(solution)/shard_map/ppermute | solution.py:294
  153.2 10.6 %all-gather.7.cloned.1.call-done.up_ref.down_ref = bf16[1152,4608]{1,0:T(8,128)(2,1)} async-done(((bf16[72,4608]{1,0:T(8,128)(2,1)}), bf16[1152,4608]{1,0:T(8,128)(2,1)}) %all-gather.7.cloned.1.call-update) | async-done | bytes 10616848 | tf_op jit(solution)/shard_map/all_gather | solution.py:333
  167.2 16.3 %shard_map.230 = (bf16[1024,2304]{1,0:T(8,128)(2,1)}, bf16[1024,2304]{1,0:T(8,128)(2,1)}, f32[1,2304]{1,0:T(1,128)S(1)}) custom-call(bf16[1024,1152]{1,0:T(8,128)(2,1)S(1)} %copy-done.1, bf16[1024,1152]{1,0:T(8,128)(2,1)S(1)} %copy-done, bf16[1152,4608]{1,0:T(8,128)(2,1)} %all-gather.7.cloned.1.call-done.up_ref.down_ref, ...), custom_call_target="tpu_custom_call" | custom-call | flops 10871635968 | bytes 24772608 | tf_op jit(solution)/shard_map/pallas_call | solution.py:196
  183.5 16.1 %shard_map.231 = bf16[1152,4608]{1,0:T(8,128)(2,1)} custom-call(bf16[1024,1152]{1,0:T(8,128)(2,1)S(1)} %copy-done, bf16[1024,1152]{1,0:T(8,128)(2,1)S(1)} %copy-done.1, bf16[1024,2304]{1,0:T(8,128)(2,1)} %get-tuple-element.67.act_ref, bf16[1024,2304]{1,0:T(8,128)(2,1)} %get-tuple-element.68.pre_ref), custom_call_target="tpu_custom_call" | custom-call | flops 10871635968 | bytes 24772608 | tf_op jit(solution)/shard_map/pallas_call | solution.py:242
  199.7 6.5 %fusion.22 = bf16[512,1152]{1,0:T(8,128)(2,1)S(1)} fusion(bf16[1152,4608]{1,0:T(8,128)(2,1)} %all-gather.7.cloned.1.call-done.up_ref.down_ref, bf16[1024,2304]{1,0:T(8,128)(2,1)} %get-tuple-element.68.pre_ref), kind=kOutput, calls=%fused_computation.27 | convolution fusion | flops 2718498816 | bytes 8847360 | tf_op jit(solution)/shard_map/dot_general | solution.py:23
  210.2 8.6 %fusion.19 = bf16[512,1152]{1,0:T(8,128)(2,1)} fusion(bf16[1152,4608]{1,0:T(8,128)(2,1)} %all-gather.7.cloned.1.call-done.up_ref.down_ref, bf16[1024,2304]{1,0:T(8,128)(2,1)} %get-tuple-element.67.act_ref), kind=kOutput, calls=%fused_computation.26 | convolution fusion | flops 2718498816 | bytes 8847360 | tf_op jit(solution)/shard_map/dot_general | solution.py:23
  218.8 15.6 %collective-permute-done.5 = bf16[512,1152]{1,0:T(8,128)(2,1)S(1)} collective-permute-done((bf16[512,1152]{1,0:T(8,128)(2,1)S(1)}, bf16[512,1152]{1,0:T(8,128)(2,1)S(1)}, u32[]{:S(2)}, u32[]{:S(2)}) %collective-permute-start.5) | collective-permute-done | bytes 1179680 | tf_op jit(solution)/shard_map/ppermute | solution.py:294
  234.4 5.2 %multiply_reduce_fusion = (f32[1152]{0:T(1024)S(1)}, f32[512]{0:T(512)S(1)}, f32[512]{0:T(512)S(1)}, f32[1152]{0:T(1024)S(1)}, f32[512,1152]{1,0:T(8,128)S(1)}) fusion(f32[512,1152]{1,0:T(8,128)S(1)} %copy-done.9, f32[512]{0:T(512)S(1)} %add_rsqrt_fusion.2, f32[512]{0:T(512)S(1)} %broadcast_multiply_fusion.6, f32[1152]{0:T(1024)S(1)} %copy-done.28, ...), kind=kOutput, calls=%fused_computation.50 | convolution fusion | flops 2724393984 | bytes 13591552 | tf_op jit(solution)/shard_map/dot_general | solution.py:23
  239.6 2.9 multiply_reduce_fusion.1
  244.3 6.3 %fusion.12 = f32[512,1152]{1,0:T(8,128)} fusion(bf16[1152,4608]{1,0:T(8,128)(2,1)S(1)} %bitcast.43, bf16[1024,2304]{1,0:T(8,128)(2,1)} %get-tuple-element.67.act_ref), kind=kOutput, calls=%fused_computation.15 | convolution fusion | flops 2717908992 | bytes 10027008 | tf_op jit(solution)/shard_map/dot_general | solution.py:23
  250.7 16.3 %shard_map.232 = (bf16[512,576]{1,0:T(8,128)(2,1)S(1)}, f32[1024,576]{1,0:T(8,128)}, f32[1024,576]{1,0:T(8,128)}) custom-call(bf16[1024,1728]{1,0:T(8,128)(2,1)} %copy-done.4, bf16[512,1152]{1,0:T(8,128)(2,1)S(1)} %get-tuple-element.162.refs_1_, bf16[1152,576]{1,0:T(8,128)(2,1)S(1)} %slice.148.refs_2_, bf16[512,576]{1,0:T(8,128)(2,1)S(1)} %copy-done.3, ...), custom_call_target="tpu_custom_call" | custom-call | flops 10737418240 | bytes 10027008 | tf_op jit(solution)/shard_map/pallas_call | solution.py:160
  267.0 3.3 collective-permute-done.6.refs_1_
  272.0 18.4 %shard_map.233 = (bf16[1024,1728]{1,0:T(8,128)(2,1)}, f32[1,1728]{1,0:T(1,128)S(1)}) custom-call(bf16[1024,1728]{1,0:T(8,128)(2,1)} %copy-done.4, bf16[512,1152]{1,0:T(8,128)(2,1)S(1)} %collective-permute-done.6.refs_1_, bf16[1152,576]{1,0:T(8,128)(2,1)S(1)} %slice.148.refs_2_, bf16[512,576]{1,0:T(8,128)(2,1)S(1)} %get-tuple-element.61.refs_3_, ...), custom_call_target="tpu_custom_call" | custom-call | flops 10737418240 | bytes 10027008 | tf_op jit(solution)/shard_map/pallas_call | solution.py:160
  290.4 11.4 %shard_map.234 = bf16[1152,2304]{1,0:T(8,128)(2,1)} custom-call(bf16[1024,1152]{1,0:T(8,128)(2,1)S(1)} %fusion.5.first_ref, bf16[1024,1728]{1,0:T(8,128)(2,1)} %get-tuple-element.77.packed_ref, bf16[1024,1152]{1,0:T(8,128)(2,1)S(1)} %pad_maximum_fusion.3.upstream_ref, bf16[1024,576]{1,0:T(8,128)(2,1)S(1)} %pad_maximum_fusion.4.heads_ref), custom_call_target="tpu_custom_call" | custom-call | flops 5435817984 | bytes 14745600 | tf_op jit(solution)/shard_map/pallas_call | solution.py:279
  304.5 11.4 %fusion.6 = (f32[1152]{0:T(1024)S(1)}, f32[1152]{0:T(1024)S(1)}, f32[1024,1152]{1,0:T(8,128)}) fusion(f32[1024]{0:T(1024)S(1)} %copy-done.39, f32[1024]{0:T(1024)S(1)} %copy-done.30, bf16[512,1152]{1,0:T(8,128)(2,1)S(1)} %copy-done.16, bf16[512,1152]{1,0:T(8,128)(2,1)S(1)} %copy-done.7, bf16[1024,1728]{1,0:T(8,128)(2,1)} %get-tuple-element.77.packed_ref, ...), kind=kOutput, calls=%fused_computation.9 | convolution fusion | flops 4087478272 | bytes 14894080 | tf_op jit(solution)/shard_map/dot_general | solution.py:23
  329.3 4.5 %all-to-all-start.2 = ((f32[16,1,9792]{2,1,0:T(1,128)}), f32[16,1,9792]{2,1,0:T(1,128)S(1)}, u32[]{:S(2)}, u32[]{:S(2)}) async-start(f32[16,1,9792]{2,1,0:T(1,128)} %broadcast_in_dim.53), calls=%async_computation.2 | async-start | bytes 1261568 | tf_op jit(solution)/shard_map/all_to_all | solution.py:338
  334.3 15.6 %all-to-all-done.2 = f32[16,1,9792]{2,1,0:T(1,128)S(1)} async-done(((f32[16,1,9792]{2,1,0:T(1,128)}), f32[16,1,9792]{2,1,0:T(1,128)S(1)}, u32[]{:S(2)}, u32[]{:S(2)}) %all-to-all-start.2) | async-done | bytes 626720 | tf_op jit(solution)/shard_map/all_to_all | solution.py:338
  350.0 2.9 collective-permute-done.9
  364.6 2.4 slice_bitcast_fusion
  371.8 4.8 %all-to-all-start.3 = ((f32[16,1,72]{2,1,0:T(1,128)}), f32[16,1,72]{2,1,0:T(1,128)S(1)}, u32[]{:S(2)}, u32[]{:S(2)}) async-start(f32[16,1,72]{2,1,0:T(1,128)} %bitcast.6), calls=%async_computation.4 | async-start | bytes 16384 | tf_op jit(solution)/shard_map/all_to_all | solution.py:338
  379.3 3.7 all-to-all-done.3
  385.5 15.9 %reduce-scatter.5.cloned.1.call-done = bf16[72,2304]{1,0:T(8,128)(2,1)} async-done(((bf16[1152,2304]{1,0:T(8,128)(2,1)}), bf16[72,2304]{1,0:T(8,128)(2,1)}) %reduce-scatter.5.cloned.1.call-update) | async-done | bytes 331792 | tf_op jit(solution)/shard_map/reduce_scatter | solution.py:474
  (217 shorter events, 81.5 us)
Async XLA Ops:
  7.2 14.2 %copy-start.24 = (bf16[72,6,576]{2,0,1:T(8,128)(2,1)S(1)}, bf16[72,6,576]{2,0,1:T(8,128)(2,1)}, u32[]{:S(2)}) copy-start(bf16[72,6,576]{2,0,1:T(8,128)(2,1)} %param.15) | copy-start | bytes 1492996
  7.2 66.5 %all-gather.5.cloned.1.call-start = ((), (), s32[]{:S(2)}) async-start(), calls=%async_computation.8 | async-start | bytes 5640192 | tf_op jit(solution)/shard_map/all_gather | solution.py:333
  10.4 31.3 %collective-permute-start = (bf16[512,1152]{1,0:T(8,128)(2,1)}, bf16[512,1152]{1,0:T(8,128)(2,1)S(1)}, u32[]{:S(2)}, u32[]{:S(2)}) collective-permute-start(bf16[512,1152]{1,0:T(8,128)(2,1)} %param.13), channel_id=1, source_target_pairs={{0,1},{1,0},{2,3},{3,2},{4,5},{5,4},{6,7},{7,6},{8,9},{9,8},{10,11... | collective-permute-start | bytes 3538952 | tf_op jit(solution)/shard_map/ppermute | solution.py:294
  15.4 12.3 %all-to-all-start = ((bf16[16,1,72]{2,1,0:T(2,128)(2,1)}), bf16[16,1,72]{2,1,0:T(2,128)(2,1)S(1)}, u32[]{:S(2)}, u32[]{:S(2)}) async-start(bf16[16,1,72]{2,1,0:T(2,128)(2,1)} %transpose_reshape.4), calls=%async_computation | async-start | bytes 16384 | tf_op jit(solution)/shard_map/all_to_all | solution.py:338
  21.3 142.5 %all-gather.7.cloned.1.call-start = ((), (), s32[]{:S(2)}) async-start(), calls=%async_computation.9 | async-start | bytes 11280384 | tf_op jit(solution)/shard_map/all_gather | solution.py:333
  22.0 26.9 %copy-start.17 = (bf16[72,3456]{1,0:T(8,128)(2,1)}, bf16[72,3456]{1,0:T(8,128)(2,1)S(1)}, u32[]{:S(2)}) copy-start(bf16[72,3456]{1,0:T(8,128)(2,1)S(1)} %reshape.172) | copy-start | bytes 1492996
  22.0 24.3 %copy-start.43 = (bf16[2,576]{1,0:T(2,128)(2,1)S(1)}, bf16[2,576]{1,0:T(2,128)(2,1)}, u32[]{:S(2)}) copy-start(bf16[2,576]{1,0:T(2,128)(2,1)} %param.18) | copy-start | bytes 6916
  22.0 26.5 %copy-start.5 = (bf16[512,1152]{1,0:T(8,128)(2,1)S(1)}, bf16[512,1152]{1,0:T(8,128)(2,1)}, u32[]{:S(2)}) copy-start(bf16[512,1152]{1,0:T(8,128)(2,1)} %param.13) | copy-start | bytes 3538948
  27.7 21.2 %copy-start.33 = (bf16[16,1,72]{2,1,0:T(2,128)(2,1)}, bf16[16,1,72]{2,1,0:T(2,128)(2,1)S(1)}, u32[]{:S(2)}) copy-start(bf16[16,1,72]{2,1,0:T(2,128)(2,1)S(1)} %all-to-all-done) | copy-start | bytes 6916
  42.4 3.8 collective-permute-start.1
  46.3 271.9 %reduce-scatter.3.cloned.1.call-start = ((), (), s32[]{:S(2)}) async-start(), calls=%async_computation.6 | async-start | bytes 11280384 | tf_op jit(solution)/shard_map/reduce_scatter | solution.py:474
  47.0 34.2 %collective-permute-start.2 = (bf16[512,1152]{1,0:T(8,128)(2,1)}, bf16[512,1152]{1,0:T(8,128)(2,1)}, u32[]{:S(2)}, u32[]{:S(2)}) collective-permute-start(bf16[512,1152]{1,0:T(8,128)(2,1)} %param.25), channel_id=1, source_target_pairs={{0,1},{1,0},{2,3},{3,2},{4,5},{5,4},{6,7},{7,6},{8,9},{9,8},{10,11... | collective-permute-start | bytes 3538952 | tf_op jit(solution)/shard_map/ppermute | solution.py:294
  91.5 28.4 %collective-permute-start.3 = (bf16[512,1152]{1,0:T(8,128)(2,1)}, bf16[512,1152]{1,0:T(8,128)(2,1)S(1)}, u32[]{:S(2)}, u32[]{:S(2)}) collective-permute-start(bf16[512,1152]{1,0:T(8,128)(2,1)} %convolution_convert_fusion), channel_id=1, source_target_pairs={{0,1},{1,0},{2,3},{3,2},{4,5},{5,4},{6,7},{7,6},{8,9},{9,8},{10,11... | collective-permute-start | bytes 3538952 | tf_op jit(solution)/shard_map/ppermute | solution.py:294
  93.2 26.6 %copy-start.35 = (f32[512]{0:T(512)}, f32[512]{0:T(512)S(1)}, u32[]{:S(2)}) copy-start(f32[512]{0:T(512)S(1)} %broadcast_multiply_fusion.3) | copy-start | bytes 6148
  93.2 26.6 %copy-start.31 = (f32[1152]{0:T(1024)S(1)}, f32[1152]{0:T(1024)}, u32[]{:S(2)}) copy-start(f32[1152]{0:T(1024)} %get-tuple-element.156) | copy-start | bytes 13828
  101.4 21.4 %copy-start.2 = (bf16[512,576]{1,0:T(8,128)(2,1)}, bf16[512,576]{1,0:T(8,128)(2,1)S(1)}, u32[]{:S(2)}) copy-start(bf16[512,576]{1,0:T(8,128)(2,1)S(1)} %get-tuple-element.60.refs_3_) | copy-start | bytes 1769476
  124.2 27.4 %collective-permute-start.4 = (bf16[512,1152]{1,0:T(8,128)(2,1)S(1)}, bf16[512,1152]{1,0:T(8,128)(2,1)S(1)}, u32[]{:S(2)}, u32[]{:S(2)}) collective-permute-start(bf16[512,1152]{1,0:T(8,128)(2,1)S(1)} %add_convert_fusion.2), channel_id=1, source_target_pairs={{0,1},{1,0},{2,3},{3,2},{4,5},{5,4},{6,7},{7,6},{8,9},{9,8},{10,11... | collective-permute-start | bytes 3538952 | tf_op jit(solution)/shard_map/ppermute | solution.py:294
  199.6 201.8 %reduce-scatter.5.cloned.1.call-start = ((), (), s32[]{:S(2)}) async-start(), calls=%async_computation.7 | async-start | bytes 5640192 | tf_op jit(solution)/shard_map/reduce_scatter | solution.py:474
  206.2 28.2 %collective-permute-start.5 = (bf16[512,1152]{1,0:T(8,128)(2,1)S(1)}, bf16[512,1152]{1,0:T(8,128)(2,1)S(1)}, u32[]{:S(2)}, u32[]{:S(2)}) collective-permute-start(bf16[512,1152]{1,0:T(8,128)(2,1)S(1)} %fusion.22), channel_id=1, source_target_pairs={{0,1},{1,0},{2,3},{3,2},{4,5},{5,4},{6,7},{7,6},{8,9},{9,8},{10,11... | collective-permute-start | bytes 3538952 | tf_op jit(solution)/shard_map/ppermute | solution.py:294
  210.0 24.4 %slice-start = ((s8[10616832]{0:T(1024)(128)(4,1)}), s8[4194304]{0:T(1024)(128)(4,1)S(1)}, s32[]{:S(2)}) async-start(s8[10616832]{0:T(1024)(128)(4,1)} %bitcast.42), calls=%async_computation.10 | async-start | bytes 8388608
  210.1 24.2 %copy-start.9 = (f32[512,1152]{1,0:T(8,128)S(1)}, f32[512,1152]{1,0:T(8,128)}, u32[]{:S(2)}) copy-start(f32[512,1152]{1,0:T(8,128)} %copy-done.8) | copy-start | bytes 7077892
  210.1 24.2 %slice-start.1 = ((s8[10616832]{0:T(1024)(128)(4,1)}), s8[4194304]{0:T(1024)(128)(4,1)S(1)}, s32[]{:S(2)}) async-start(s8[10616832]{0:T(1024)(128)(4,1)} %bitcast.42), calls=%async_computation.11 | async-start | bytes 8388608
  210.2 24.2 %slice-start.2 = ((s8[10616832]{0:T(1024)(128)(4,1)}), s8[2228224]{0:T(1024)(128)(4,1)S(1)}, s32[]{:S(2)}) async-start(s8[10616832]{0:T(1024)(128)(4,1)} %bitcast.42), calls=%async_computation.12 | async-start | bytes 4456448
  218.8 20.8 %copy-start.20 = (f32[512,1152]{1,0:T(8,128)S(1)}, f32[512,1152]{1,0:T(8,128)}, u32[]{:S(2)}) copy-start(f32[512,1152]{1,0:T(8,128)} %get-tuple-element.179) | copy-start | bytes 7077892
  218.8 20.8 %copy-start.23 = (bf16[512,1152]{1,0:T(8,128)(2,1)S(1)}, bf16[512,1152]{1,0:T(8,128)(2,1)}, u32[]{:S(2)}) copy-start(bf16[512,1152]{1,0:T(8,128)(2,1)} %copy-done.22) | copy-start | bytes 3538948
  242.8 27.5 %collective-permute-start.6 = (bf16[512,1152]{1,0:T(8,128)(2,1)S(1)}, bf16[512,1152]{1,0:T(8,128)(2,1)S(1)}, u32[]{:S(2)}, u32[]{:S(2)}) collective-permute-start(bf16[512,1152]{1,0:T(8,128)(2,1)S(1)} %get-tuple-element.162.refs_1_), channel_id=1, source_target_pairs={{0,1},{1,0},{2,3},{3,2},{4,5},{5,4},{6,7},{7,6},{8,9},{9,8},{10,11... | collective-permute-start | bytes 3538952 | tf_op jit(solution)/shard_map/ppermute | solution.py:294
  270.3 31.5 %collective-permute-start.7 = (bf16[512,1152]{1,0:T(8,128)(2,1)}, bf16[512,1152]{1,0:T(8,128)(2,1)}, u32[]{:S(2)}, u32[]{:S(2)}) collective-permute-start(bf16[512,1152]{1,0:T(8,128)(2,1)} %fusion.19), channel_id=1, source_target_pairs={{0,1},{1,0},{2,3},{3,2},{4,5},{5,4},{6,7},{7,6},{8,9},{9,8},{10,11... | collective-permute-start | bytes 3538952 | tf_op jit(solution)/shard_map/ppermute | solution.py:294
  320.5 4.0 collective-permute-start.8
  326.3 26.6 %collective-permute-start.9 = (bf16[512,1152]{1,0:T(8,128)(2,1)S(1)}, bf16[512,1152]{1,0:T(8,128)(2,1)}, u32[]{:S(2)}, u32[]{:S(2)}) collective-permute-start(bf16[512,1152]{1,0:T(8,128)(2,1)S(1)} %slice.217), channel_id=1, source_target_pairs={{0,1},{1,0},{2,3},{3,2},{4,5},{5,4},{6,7},{7,6},{8,9},{9,8},{10,11... | collective-permute-start | bytes 3538952 | tf_op jit(solution)/shard_map/ppermute | solution.py:294
  329.3 20.7 %all-to-all-start.2 = ((f32[16,1,9792]{2,1,0:T(1,128)}), f32[16,1,9792]{2,1,0:T(1,128)S(1)}, u32[]{:S(2)}, u32[]{:S(2)}) async-start(f32[16,1,9792]{2,1,0:T(1,128)} %broadcast_in_dim.53), calls=%async_computation.2 | async-start | bytes 1261568 | tf_op jit(solution)/shard_map/all_to_all | solution.py:338
  356.0 14.4 %collective-permute-start.10 = (f32[16,72]{1,0:T(8,128)}, f32[16,72]{1,0:T(8,128)}, u32[]{:S(2)}, u32[]{:S(2)}) collective-permute-start(f32[16,72]{1,0:T(8,128)} %fusion.51), channel_id=1, source_target_pairs={{0,1},{1,0},{2,3},{3,2},{4,5},{5,4},{6,7},{7,6},{8,9},{9,8},{10,11... | collective-permute-start | bytes 13832 | tf_op jit(solution)/shard_map/ppermute | solution.py:294
  371.8 11.2 %all-to-all-start.3 = ((f32[16,1,72]{2,1,0:T(1,128)}), f32[16,1,72]{2,1,0:T(1,128)S(1)}, u32[]{:S(2)}, u32[]{:S(2)}) async-start(f32[16,1,72]{2,1,0:T(1,128)} %bitcast.6), calls=%async_computation.4 | async-start | bytes 16384 | tf_op jit(solution)/shard_map/all_to_all | solution.py:338
  (33 other events, 142.2 us)
Sparse Core Ops, SparseCore 0:
  10.8 62.9 all-gather.4
  76.6 87.2 all-gather.6
  199.8 118.3 reduce-scatter.2
  322.1 79.3 reduce-scatter.4
